TPU v7x, 128 devices: a whole 4x4x4 slice. The times are simulated.
128 devices in a mesh: tx: 8 (over x, core), ty: 16 (over z, y).
Axes of the slice: x: 4, y: 4, z: 4, core: 2. Of those that a mesh axis runs over, the one named last changes fastest.
Arguments:
- cot_field: float32 [8, 2048, 8192], P(None, 'tx', 'ty'), may hold values from -6 to 6
- conductance: float32 [8, 2048, 8192], P(None, 'tx', 'ty'), may hold values from 0.04 to 0.16
- diagonal: float32 [8, 2048, 8192], P(None, 'tx', 'ty'), may hold values from 1 to 2
- source_adjoint: bfloat16 [262144, 128], P(('tx', 'ty')), may hold values from -6 to 6
- spreading: bfloat16 [16, 128, 128], replicated, may hold values from -0.5 to 0.5
- heat_deriv: float32 [262144, 128], P(('tx', 'ty')), may hold values from 0.25 to 1.75
- block_tile: int32 [262144, 1], P(('tx', 'ty')), may hold values from 0 to 127; in each aligned block of 2048 rows (0 to 2047, 2048 to 4095, ...) at most 32 rows name the same one
- block_patch: int32 [262144], P(('tx', 'ty')), may hold values from 0 to 8191
- block_kind: int32 [262144], P(('tx', 'ty')), may hold values from 0 to 15
Outputs:
- temp_adjoint: float32 [8, 2048, 8192], P(None, 'tx', 'ty')
- source_grad: float32 [262144, 128], P(('tx', 'ty'))
Inputs may be any that keep to these rules, and one draw needn't show every extreme that they name: `block_tile`: among the blocks of one device, no tile is named by more than 32 blocks, a bound that some block reaches.
All inputs are finite; a program needn't handle non-finite values.
Results may differ from a plain program's by a relative error of at most 0.0018.
The roundings to bfloat16 on the way count: a program that leaves them out, or rounds other values in their place, can miss the bound.
Values may be sent and summed in bfloat16 or wider, within the bound.
A program may use at most 128 MiB of HBM per device.

v0:
```python
import jax
import jax.numpy as jnp
from jax import lax
from jax.sharding import PartitionSpec as P

SWEEPS = 2


def padded_2(value, sides, width):
    for axis, dim in sides:
        size, length = (lax.axis_size(axis), value.shape[dim])
        up = [(i, (i + 1) % size) for i in range(size - 1)]
        down = [(j, i) for i, j in up]
        last = lax.slice_in_dim(value, length - width, length, axis=dim)
        leading = lax.slice_in_dim(value, 0, width, axis=dim)
        before = lax.ppermute(last, axis, up)
        after = lax.ppermute(leading, axis, down)
        value = jnp.concatenate([before, value, after], axis=dim)
    return value


def neighbours(padded):
    centre = padded[:, 1:-1, 1:-1]
    layered = jnp.pad(centre, ((1, 1), (0, 0), (0, 0)))
    total = padded[:, :-2, 1:-1] + padded[:, 2:, 1:-1]
    total = total + padded[:, 1:-1, :-2] + padded[:, 1:-1, 2:]
    return total + layered[:-2] + layered[2:]


def spread_rows(seeds, kinds, spreading):
    kinds_all = spreading.shape[0]
    onehot = (kinds[:, None] == jnp.arange(kinds_all, dtype=jnp.int32)[None, :]).astype(
        jnp.bfloat16
    )
    masked = (seeds[:, None, :] * onehot[:, :, None]).reshape(seeds.shape[0], kinds_all * 128)
    return jnp.dot(
        masked, spreading.reshape(kinds_all * 128, 128), preferred_element_type=jnp.float32
    )


def local(
    cot_field,
    conductance,
    diagonal,
    source_adjoint,
    spreading,
    heat_deriv,
    block_tile,
    block_patch,
    block_kind,
):
    rows_x = lax.axis_size("tx")
    rows_y = lax.axis_size("ty")
    devices = rows_x * rows_y
    owned = source_adjoint.shape[0]
    capacity = 2 * owned // devices
    kinds_all = spreading.shape[0]
    layers, tile_x, tile_y = cot_field.shape
    patches = layers * tile_x * tile_y // 128
    slots = devices * capacity
    targets = block_tile[:, 0]
    dest_hits = (targets[:, None] == jnp.arange(devices, dtype=jnp.int32)[None, :]).astype(
        jnp.int32
    )
    before = jnp.cumsum(dest_hits, axis=0) - dest_hits
    slot_number = jnp.sum(before * dest_hits, axis=1)
    slot_index = targets * capacity + slot_number
    cell_seed = spread_rows(source_adjoint, block_kind, spreading)
    send_values = jnp.zeros((slots, 128), jnp.float32).at[slot_index].set(cell_seed)
    send_ids = jnp.full((slots,), patches, jnp.int32).at[slot_index].set(block_patch)
    got_values, got_ids = (
        lax.all_to_all(
            send_values.reshape(devices, capacity, 128),
            ("tx", "ty"),
            split_axis=0,
            concat_axis=0,
            tiled=True,
        ),
        lax.all_to_all(
            send_ids.reshape(devices, capacity),
            ("tx", "ty"),
            split_axis=0,
            concat_axis=0,
            tiled=True,
        ),
    )
    got_values = got_values.reshape(slots, 128)
    got_ids = got_ids.reshape(slots)
    rhs = cot_field.reshape(patches, 128).at[got_ids].add(got_values, mode="drop")
    rhs = rhs.reshape(layers, tile_x, tile_y)
    inverse_diag = 1.0 / diagonal
    adjoint = rhs * inverse_diag
    for sweep_index in range(SWEEPS):
        padded = padded_2(conductance * adjoint, (("tx", 1), ("ty", 2)), 1)
        adjoint = (rhs + neighbours(padded)) * inverse_diag
    heat_rows = jnp.take(adjoint.reshape(patches, 128), got_ids, axis=0, mode="clip").astype(
        jnp.bfloat16
    )
    returned = lax.all_to_all(
        heat_rows.reshape(devices, capacity, 128),
        ("tx", "ty"),
        split_axis=0,
        concat_axis=0,
        tiled=True,
    )
    heat_patch = returned.reshape(slots, 128)[slot_index]
    onehot = block_kind[:, None] == jnp.arange(kinds_all, dtype=jnp.int32)[None, :]
    stacked_t = jnp.transpose(spreading, (2, 0, 1)).reshape(128, kinds_all * 128)
    pulled_all = jnp.dot(heat_patch, stacked_t, preferred_element_type=jnp.float32).reshape(
        owned, kinds_all, 128
    )
    pulled = jnp.sum(pulled_all * onehot.astype(jnp.float32)[:, :, None], axis=1)
    source_grad = heat_deriv * pulled
    return (adjoint, source_grad)


def solution(mesh):
    in_specs = (
        P(None, "tx", "ty"),
        P(None, "tx", "ty"),
        P(None, "tx", "ty"),
        P(("tx", "ty"), None),
        P(),
        P(("tx", "ty"), None),
        P(("tx", "ty"), None),
        P(("tx", "ty")),
        P(("tx", "ty")),
    )
    out_specs = (P(None, "tx", "ty"), P(("tx", "ty"), None))
    return jax.shard_map(local, mesh=mesh, in_specs=in_specs, out_specs=out_specs, check_vma=False)
```

profile of v0, /device:TPU:1, one launch (start us, length us, event | category | flops | bytes accessed | tf_op | source)
XLA Modules:
  0.0 240.7 jit_solution(11966087194326019602)
XLA Ops:
  3.0 8.2 %scatter_custom_fusion = s32[4096]{0:T(1024)S(1)} fusion(s32[2048]{0:T(1024)S(1)} %bitcast.46, s32[2048]{0:T(1024)} %param.16, s32[]{:T(128)} %constant.6.clone.1), kind=kCustom, calls=%fused_computation.73 | custom fusion | bytes 16896 | tf_op jit(solution)/shard_map/scatter | solution.py:70
  12.0 11.5 %all-to-all-start = ((s32[128,1,32]{2,1,0:T(1,128)}), s32[128,1,32]{2,1,0:T(1,128)S(1)}, u32[]{:S(2)}, u32[]{:S(2)}) async-start(s32[128,1,32]{2,1,0:T(1,128)} %bitcast.7), calls=%async_computation | async-start | bytes 131072 | tf_op jit(solution)/shard_map/all_to_all | solution.py:79
  23.5 4.6 %fusion.19 = f32[2048,128]{1,0:T(8,128)S(1)} fusion(bf16[16,128,128]{2,1,0:T(8,128)(2,1)S(1)} %copy-done, bf16[2048,16]{0,1:T(8,128)(2,1)S(1)} %get-tuple-element.13, bf16[2048,128]{1,0:T(8,128)(2,1)S(1)} %copy-done.6), kind=kOutput, calls=%fused_computation.46 | convolution fusion | flops 1077936128 | bytes 2162688 | tf_op jit(solution)/shard_map/dot_general | solution.py:36
  28.1 7.0 %scatter_custom_fusion.1 = f32[4096,128]{1,0:T(8,128)} fusion(s32[2048]{0:T(1024)S(1)} %bitcast.47, f32[2048,128]{1,0:T(8,128)S(1)} %fusion.19, f32[]{:T(128)} %constant.4.clone.1), kind=kCustom, calls=%fused_computation.57 | custom fusion | bytes 2097156 | tf_op jit(solution)/shard_map/scatter | solution.py:69
  35.1 9.8 %all-to-all-start.1 = ((f32[128,32,128]{2,1,0:T(8,128)}), f32[128,32,128]{2,1,0:T(8,128)S(1)}, u32[]{:S(2)}, u32[]{:S(2)}) async-start(f32[128,32,128]{2,1,0:T(8,128)} %bitcast.39), calls=%async_computation.1 | async-start | bytes 4194304 | tf_op jit(solution)/shard_map/all_to_all | solution.py:72
  44.9 4.7 %reshape.128 = f32[8192,128]{1,0:T(8,128)} reshape(f32[8,256,512]{2,1,0:T(8,128)} %param.9) | data formatting | bytes 8388608 | tf_op jit(solution)/shard_map/reshape | solution.py:89
  51.1 23.1 %all-to-all-done.1 = f32[128,32,128]{2,1,0:T(8,128)S(1)} async-done(((f32[128,32,128]{2,1,0:T(8,128)}), f32[128,32,128]{2,1,0:T(8,128)S(1)}, u32[]{:S(2)}, u32[]{:S(2)}) %all-to-all-start.1) | async-done | bytes 2097184 | tf_op jit(solution)/shard_map/all_to_all | solution.py:72
  74.2 24.3 %scatter_fusion = f32[8192,128]{1,0:T(8,128)} fusion(f32[8192,128]{1,0:T(8,128)} %reshape.128, s32[4096]{0:T(1024)S(1)} %bitcast.44, f32[4096,128]{1,0:T(8,128)S(1)} %bitcast.38), kind=kCustom, calls=%fused_computation.4 | custom fusion | flops 524288 | bytes 6307840 | tf_op jit(solution)/shard_map/scatter-add | solution.py:89
  98.4 4.9 %reshape.133 = f32[8,256,512]{2,1,0:T(8,128)} reshape(f32[8192,128]{1,0:T(8,128)} %scatter_fusion) | data formatting | bytes 8388608 | tf_op jit(solution)/shard_map/reshape | solution.py:90
  103.3 6.2 %multiply_multiply_fusion = f32[8,256,512]{2,1,0:T(8,128)S(1)} fusion(f32[8,256,512]{2,1,0:T(8,128)} %param.10, f32[8,256,512]{2,1,0:T(8,128)} %reshape.133, f32[8,256,512]{2,1,0:T(8,128)} %param.11), kind=kLoop, calls=%fused_computation.43 | loop fusion | flops 3145728 | bytes 16777216 | tf_op jit(solution)/shard_map/mul | solution.py:94
  109.6 4.0 %collective-permute-start = (f32[8,1,512]{2,1,0:T(1,128)S(1)}, f32[8,1,512]{2,1,0:T(1,128)S(1)}, u32[]{:S(2)}, u32[]{:S(2)}) collective-permute-start(f32[8,1,512]{2,1,0:T(1,128)S(1)} %get-tuple-element.10), channel_id=1, source_target_pairs={{0,16},{16,32},{32,48},{48,64},{64,80},{80,96},{96,112},{1,17},{17... | collective-permute-start | bytes 49160 | tf_op jit(solution)/shard_map/ppermute | solution.py:16
  115.5 3.1 %collective-permute-done.1 = f32[8,1,512]{2,1,0:T(1,128)S(1)} collective-permute-done((f32[8,1,512]{2,1,0:T(1,128)S(1)}, f32[8,1,512]{2,1,0:T(1,128)S(1)}, u32[]{:S(2)}, u32[]{:S(2)}) %collective-permute-start.1) | collective-permute-done | bytes 16416 | tf_op jit(solution)/shard_map/ppermute | solution.py:17
  124.0 2.7 %collective-permute-done.3 = f32[8,258,1]{1,0,2:T(8,128)S(1)} collective-permute-done((f32[8,258,1]{1,0,2:T(8,128)S(1)}, f32[8,258,1]{1,0,2:T(8,128)S(1)}, u32[]{:S(2)}, u32[]{:S(2)}) %collective-permute-start.3) | collective-permute-done | bytes 8288 | tf_op jit(solution)/shard_map/ppermute | solution.py:17
  127.2 15.9 %fusion.6 = f32[8,256,512]{2,1,0:T(8,128)S(1)} fusion(f32[8,256,512]{2,1,0:T(8,128)} %param.10, f32[8,256,512]{2,1,0:T(8,128)} %reshape.133, f32[8,256,512]{2,1,0:T(8,128)} %copy-done.2, f32[8,258,1]{2,1,0:T(8,128)S(1)} %copy.28, f32[8,1,512]{2,1,0:T(1,128)S(1)} %collective-permute-done.1, f32[8,1,512]{2,1,0:T(1,128)S(1)} %collective-permute-done, ...), kind=kLoop, calls=%fused_computation.16 | loop fusion | flops 17825792 | bytes 21020800 | tf_op jit(solution)/shard_map/mul | solution.py:94
  145.1 3.4 %collective-permute-start.4 = (f32[8,1,512]{2,1,0:T(1,128)S(1)}, f32[8,1,512]{2,1,0:T(1,128)S(1)}, u32[]{:S(2)}, u32[]{:S(2)}) collective-permute-start(f32[8,1,512]{2,1,0:T(1,128)S(1)} %get-tuple-element.8), channel_id=1, source_target_pairs={{0,16},{16,32},{32,48},{48,64},{64,80},{80,96},{96,112},{1,17},{17... | collective-permute-start | bytes 49160 | tf_op jit(solution)/shard_map/ppermute | solution.py:16
  150.5 3.0 %collective-permute-done.5 = f32[8,1,512]{2,1,0:T(1,128)S(1)} collective-permute-done((f32[8,1,512]{2,1,0:T(1,128)S(1)}, f32[8,1,512]{2,1,0:T(1,128)S(1)}, u32[]{:S(2)}, u32[]{:S(2)}) %collective-permute-start.5) | collective-permute-done | bytes 16416 | tf_op jit(solution)/shard_map/ppermute | solution.py:17
  157.8 4.2 %collective-permute-start.6 = (f32[8,258,1]{1,0,2:T(8,128)S(1)}, f32[8,258,1]{1,0,2:T(8,128)S(1)}, u32[]{:S(2)}, u32[]{:S(2)}) collective-permute-start(f32[8,258,1]{1,0,2:T(8,128)S(1)} %copy.29), channel_id=1, source_target_pairs={{0,1},{1,2},{2,3},{3,4},{4,5},{5,6},{6,7},{7,8},{8,9},{9,10},{10,1... | collective-permute-start | bytes 24776 | tf_op jit(solution)/shard_map/ppermute | solution.py:16
  163.4 15.5 %fusion.10 = f32[8,256,512]{2,1,0:T(8,128)} fusion(f32[8,256,512]{2,1,0:T(8,128)} %reshape.133, f32[8,256,512]{2,1,0:T(8,128)} %copy-done.1, f32[8,258,1]{2,1,0:T(8,128)S(1)} %copy.32, f32[8,1,512]{2,1,0:T(1,128)S(1)} %collective-permute-done.5, f32[8,1,512]{2,1,0:T(1,128)S(1)} %collective-permute-done.4, f32[8,258,1]{2,1,0:T(8,128)S(1)} %copy.30, ...), kind=kLoop, calls=%fused_computation.20 | loop fusion | flops 16777216 | bytes 16826496 | tf_op jit(solution)/shard_map/mul | solution.py:95
  178.9 3.4 %reshape.134 = bf16[8192,128]{1,0:T(8,128)(2,1)S(1)} reshape(f32[8,256,512]{2,1,0:T(8,128)} %fusion.10) | data formatting | bytes 6291456 | tf_op jit(solution)/shard_map/reshape | solution.py:96
  182.3 15.0 %gather_fusion = bf16[4096,128]{1,0:T(8,128)(2,1)} fusion(bf16[8192,128]{1,0:T(8,128)(2,1)S(1)} %reshape.134, s32[4096]{0:T(1024)S(1)} %broadcast_clamp_fusion), kind=kCustom, calls=%fused_computation | custom fusion | bytes 2113536 | tf_op jit(solution)/shard_map/jit(_take)/gather | solution.py:96
  197.4 12.0 %all-to-all-start.2 = ((bf16[128,32,128]{2,1,0:T(8,128)(2,1)}), bf16[128,32,128]{2,1,0:T(8,128)(2,1)S(1)}, u32[]{:S(2)}, u32[]{:S(2)}) async-start(bf16[128,32,128]{2,1,0:T(8,128)(2,1)} %bitcast.40), calls=%async_computation.2 | async-start | bytes 2097152 | tf_op jit(solution)/shard_map/all_to_all | solution.py:99
  209.4 18.8 %all-to-all-done.2 = bf16[128,32,128]{2,1,0:T(8,128)(2,1)S(1)} async-done(((bf16[128,32,128]{2,1,0:T(8,128)(2,1)}), bf16[128,32,128]{2,1,0:T(8,128)(2,1)S(1)}, u32[]{:S(2)}, u32[]{:S(2)}) %all-to-all-start.2) | async-done | bytes 1048608 | tf_op jit(solution)/shard_map/all_to_all | solution.py:99
  228.3 6.2 %gather_fusion.1 = bf16[2048,128]{1,0:T(8,128)(2,1)S(1)} fusion(bf16[4096,128]{1,0:T(8,128)(2,1)S(1)} %bitcast.37, s32[2048]{0:T(1024)S(1)} %broadcast_clamp_fusion.1), kind=kCustom, calls=%fused_computation.1 | custom fusion | bytes 1056768 | tf_op jit(solution)/shard_map/gather | solution.py:106
  234.4 5.2 %multiply_reduce_fusion = f32[2048,128]{1,0:T(8,128)S(1)} fusion(f32[2048,16]{0,1:T(8,128)S(1)} %get-tuple-element.12, bf16[16,128,128]{2,1,0:T(8,128)(2,1)S(1)} %copy-done, bf16[2048,128]{1,0:T(8,128)(2,1)S(1)} %gather_fusion.1), kind=kOutput, calls=%fused_computation.5 | convolution fusion | flops 1081868288 | bytes 2228224 | tf_op jit(solution)/shard_map/dot_general | solution.py:109
  (56 shorter events, 22.8 us)
Async XLA Ops:
  0.6 22.9 %copy-start = (bf16[16,128,128]{2,1,0:T(8,128)(2,1)S(1)}, bf16[16,128,128]{2,1,0:T(8,128)(2,1)}, u32[]{:S(2)}) copy-start(bf16[16,128,128]{2,1,0:T(8,128)(2,1)} %param.13) | copy-start | bytes 1572868
  0.6 1.7 copy-start.4
  0.7 22.8 %copy-start.5 = (s32[2048]{0:T(1024)S(1)}, s32[2048]{0:T(1024)}, u32[]{:S(2)}) copy-start(s32[2048]{0:T(1024)} %param.17) | copy-start | bytes 24580
  0.7 22.9 %copy-start.6 = (bf16[2048,128]{1,0:T(8,128)(2,1)S(1)}, bf16[2048,128]{1,0:T(8,128)(2,1)}, u32[]{:S(2)}) copy-start(bf16[2048,128]{1,0:T(8,128)(2,1)} %param.12) | copy-start | bytes 1572868
  12.0 23.1 %all-to-all-start = ((s32[128,1,32]{2,1,0:T(1,128)}), s32[128,1,32]{2,1,0:T(1,128)S(1)}, u32[]{:S(2)}, u32[]{:S(2)}) async-start(s32[128,1,32]{2,1,0:T(1,128)} %bitcast.7), calls=%async_computation | async-start | bytes 131072 | tf_op jit(solution)/shard_map/all_to_all | solution.py:79
  35.1 39.0 %all-to-all-start.1 = ((f32[128,32,128]{2,1,0:T(8,128)}), f32[128,32,128]{2,1,0:T(8,128)S(1)}, u32[]{:S(2)}, u32[]{:S(2)}) async-start(f32[128,32,128]{2,1,0:T(8,128)} %bitcast.39), calls=%async_computation.1 | async-start | bytes 4194304 | tf_op jit(solution)/shard_map/all_to_all | solution.py:72
  109.6 9.1 %copy-start.2 = (f32[8,256,512]{2,1,0:T(8,128)}, f32[8,256,512]{2,1,0:T(8,128)S(1)}, u32[]{:S(2)}) copy-start(f32[8,256,512]{2,1,0:T(8,128)S(1)} %multiply_multiply_fusion) | copy-start | bytes 12582916
  109.6 5.9 %collective-permute-start = (f32[8,1,512]{2,1,0:T(1,128)S(1)}, f32[8,1,512]{2,1,0:T(1,128)S(1)}, u32[]{:S(2)}, u32[]{:S(2)}) collective-permute-start(f32[8,1,512]{2,1,0:T(1,128)S(1)} %get-tuple-element.10), channel_id=1, source_target_pairs={{0,16},{16,32},{32,48},{48,64},{64,80},{80,96},{96,112},{1,17},{17... | collective-permute-start | bytes 49160 | tf_op jit(solution)/shard_map/ppermute | solution.py:16
  113.6 5.1 %collective-permute-start.1 = (f32[8,1,512]{2,1,0:T(1,128)S(1)}, f32[8,1,512]{2,1,0:T(1,128)S(1)}, u32[]{:S(2)}, u32[]{:S(2)}) collective-permute-start(f32[8,1,512]{2,1,0:T(1,128)S(1)} %get-tuple-element.11), channel_id=1, source_target_pairs={{16,0},{32,16},{48,32},{64,48},{80,64},{96,80},{112,96},{17,1},{33... | collective-permute-start | bytes 49160 | tf_op jit(solution)/shard_map/ppermute | solution.py:17
  119.6 4.1 %collective-permute-start.2 = (f32[8,258,1]{1,0,2:T(8,128)S(1)}, f32[8,258,1]{1,0,2:T(8,128)S(1)}, u32[]{:S(2)}, u32[]{:S(2)}) collective-permute-start(f32[8,258,1]{1,0,2:T(8,128)S(1)} %copy.25), channel_id=1, source_target_pairs={{0,1},{1,2},{2,3},{3,4},{4,5},{5,6},{6,7},{7,8},{8,9},{9,10},{10,1... | collective-permute-start | bytes 24776 | tf_op jit(solution)/shard_map/ppermute | solution.py:16
  122.3 4.4 %collective-permute-start.3 = (f32[8,258,1]{1,0,2:T(8,128)S(1)}, f32[8,258,1]{1,0,2:T(8,128)S(1)}, u32[]{:S(2)}, u32[]{:S(2)}) collective-permute-start(f32[8,258,1]{1,0,2:T(8,128)S(1)} %copy.27), channel_id=1, source_target_pairs={{1,0},{2,1},{3,2},{4,3},{5,4},{6,5},{7,6},{8,7},{9,8},{10,9},{11,1... | collective-permute-start | bytes 24776 | tf_op jit(solution)/shard_map/ppermute | solution.py:17
  143.1 2.0 copy-start.1
  145.1 5.4 %collective-permute-start.4 = (f32[8,1,512]{2,1,0:T(1,128)S(1)}, f32[8,1,512]{2,1,0:T(1,128)S(1)}, u32[]{:S(2)}, u32[]{:S(2)}) collective-permute-start(f32[8,1,512]{2,1,0:T(1,128)S(1)} %get-tuple-element.8), channel_id=1, source_target_pairs={{0,16},{16,32},{32,48},{48,64},{64,80},{80,96},{96,112},{1,17},{17... | collective-permute-start | bytes 49160 | tf_op jit(solution)/shard_map/ppermute | solution.py:16
  148.5 5.1 %collective-permute-start.5 = (f32[8,1,512]{2,1,0:T(1,128)S(1)}, f32[8,1,512]{2,1,0:T(1,128)S(1)}, u32[]{:S(2)}, u32[]{:S(2)}) collective-permute-start(f32[8,1,512]{2,1,0:T(1,128)S(1)} %get-tuple-element.9), channel_id=1, source_target_pairs={{16,0},{32,16},{48,32},{64,48},{80,64},{96,80},{112,96},{17,1},{33... | collective-permute-start | bytes 49160 | tf_op jit(solution)/shard_map/ppermute | solution.py:17
  156.5 6.5 %collective-permute-start.7 = (f32[8,258,1]{1,0,2:T(8,128)S(1)}, f32[8,258,1]{1,0,2:T(8,128)S(1)}, u32[]{:S(2)}, u32[]{:S(2)}) collective-permute-start(f32[8,258,1]{1,0,2:T(8,128)S(1)} %copy.31), channel_id=1, source_target_pairs={{1,0},{2,1},{3,2},{4,3},{5,4},{6,5},{7,6},{8,7},{9,8},{10,9},{11,1... | collective-permute-start | bytes 24776 | tf_op jit(solution)/shard_map/ppermute | solution.py:17
  157.8 4.8 %collective-permute-start.6 = (f32[8,258,1]{1,0,2:T(8,128)S(1)}, f32[8,258,1]{1,0,2:T(8,128)S(1)}, u32[]{:S(2)}, u32[]{:S(2)}) collective-permute-start(f32[8,258,1]{1,0,2:T(8,128)S(1)} %copy.29), channel_id=1, source_target_pairs={{0,1},{1,2},{2,3},{3,4},{4,5},{5,6},{6,7},{7,8},{8,9},{9,10},{10,1... | collective-permute-start | bytes 24776 | tf_op jit(solution)/shard_map/ppermute | solution.py:16
  197.4 30.9 %all-to-all-start.2 = ((bf16[128,32,128]{2,1,0:T(8,128)(2,1)}), bf16[128,32,128]{2,1,0:T(8,128)(2,1)S(1)}, u32[]{:S(2)}, u32[]{:S(2)}) async-start(bf16[128,32,128]{2,1,0:T(8,128)(2,1)} %bitcast.40), calls=%async_computation.2 | async-start | bytes 2097152 | tf_op jit(solution)/shard_map/all_to_all | solution.py:99
  234.4 5.2 %copy-start.3 = (f32[2048,128]{1,0:T(8,128)S(1)}, f32[2048,128]{1,0:T(8,128)}, u32[]{:S(2)}) copy-start(f32[2048,128]{1,0:T(8,128)} %param.14) | copy-start | bytes 3145732
where the time goes:
time: 242 us; the launch traced here: 241 us
  other arithmetic  67.4 us (28%)
  local copies, waits for them, and re-layouts  57.6 us (24%)
  starting transfers between devices  53.6 us (22%)
  waiting for transfers between devices  51.4 us (21%)
  matrix products  9.78 us (4%)
    scatter-add x1, other arithmetic, local(): cot_field.reshape(patches, 128).at[got_ids].add(got_values, mode='drop')  24.3 us
    all_to_all x1, waiting for transfers between devices, local(): lax.all_to_all(send_values.reshape(devices, capacity, 128), ('tx', 'ty'),...  23.1 us
    mul x2, other arithmetic, local(): padded = padded_2(conductance * adjoint, (('tx', 1), ('ty', 2)), 1)  22.2 us
    all_to_all x1, waiting for transfers between devices, local(): lax.all_to_all(heat_rows.reshape(devices, capacity, 128), ('tx', 'ty'), s...  18.8 us
    mul x1, other arithmetic, local(): adjoint = (rhs + neighbours(padded)) * inverse_diag  15.5 us
    gather x1, local copies, waits for them, and re-layouts, local(): jnp.take(adjoint.reshape(patches, 128), got_ids, axis=0, mode='clip')  15 us
    ppermute x4, starting transfers between devices, padded_2(): before = lax.ppermute(last, axis, up)  13.8 us
    all_to_all x1, starting transfers between devices, local(): lax.all_to_all(heat_rows.reshape(devices, capacity, 128), ('tx', 'ty'), s...  12 us
  transfers between devices with their start and end apart: 11, of which 6 were waited for; matrix products, arithmetic and copies ran while one was open for 8% of the time, Pallas kernels for 0%

commit v1 on v0

v1 whole, which is shorter than its diff:
```python
import functools

import jax
import jax.numpy as jnp
from jax import lax
from jax.experimental import pallas as pl
from jax.experimental.pallas import tpu as pltpu
from jax.sharding import PartitionSpec as P

NX_DEV, NY_DEV = 8, 16
DEV = NX_DEV * NY_DEV
CAP = 32
SLOTS = DEV * CAP
KINDS = 16
NZ, CX, CY = 8, 256, 512
CH = CY // 128
PATCHES = NZ * CX * CH
ROWS = PATCHES + CAP
SEG = CX + 16
GROWS = CH * (NZ + 2) * SEG
OWNED = 2048
GROUP = 8
F32, BF16, I32 = jnp.float32, jnp.bfloat16, jnp.int32
MESH = pl.DeviceIdType.MESH
VMEM = pl.BlockSpec(memory_space=pltpu.VMEM)
SMEM = pl.BlockSpec(memory_space=pltpu.SMEM)
ANY = pl.BlockSpec(memory_space=pl.ANY)
NT = (((1,), (1,)), ((), ()))


def dot(a, b):
    return jnp.dot(a, b, preferred_element_type=F32)


def iota(shape, dim):
    return lax.broadcasted_iota(I32, shape, dim)


def route_kernel(
    tile_ref, patch_ref, kind_ref, src_ref,
    send_ref, meta_ref, slot_ref, kb_ref,
    srcf, sendf, slot_s, sem,
):
    sub, lane = iota((128, 128), 0), iota((128, 128), 1)
    before = (sub < lane).astype(F32).astype(BF16)
    ones = jnp.ones((128, 128), BF16)
    rank_row = iota((CAP, 128), 0)
    count = jnp.zeros((128, 128), F32)
    table = jnp.zeros((128, 128), F32)
    for j in range(OWNED // 128):
        tile = tile_ref[j : j + 1, :]
        patch = patch_ref[j : j + 1, :]
        kind = kind_ref[j : j + 1, :]
        place = (patch & (CH - 1)) * (NZ * CX) + (patch >> 2)
        hit = (sub == tile).astype(F32)
        hit16 = hit.astype(BF16)
        rank = jnp.sum(hit * (dot(hit16, before) + count), axis=0, keepdims=True).astype(I32)
        count = count + dot(hit16, ones)
        slot_ref[j : j + 1, :] = tile * CAP + rank
        at = (rank_row == rank).astype(F32)
        parts = jnp.concatenate(
            [
                at * (place >> 7).astype(F32),
                at * (place & 127).astype(F32),
                at * (kind + 1).astype(F32),
                jnp.zeros((128 - 3 * CAP, 128), F32),
            ],
            axis=0,
        ).astype(BF16)
        table = table + lax.dot_general(hit16, parts, NT, preferred_element_type=F32)
        kb_ref[pl.ds(j * 128, 128), :] = jnp.transpose(
            jnp.broadcast_to(kind.astype(F32), (128, 128))
        ).astype(BF16)
    copy = pltpu.make_async_copy(slot_ref, slot_s, sem)
    copy.start()
    counts = count.astype(I32)
    place = (table * 128.0 + pltpu.roll(table, 128 - CAP, 1)).astype(I32)
    kind1 = pltpu.roll(table, 128 - 2 * CAP, 1).astype(I32)
    place = jnp.where(lane < counts, place, PATCHES + lane)
    within = lane & (GROUP - 1)
    clash = jnp.zeros((128, 128), I32)
    for k in range(1, GROUP):
        same = (pltpu.roll(place, k, 1) == place) & (within >= k)
        clash = jnp.maximum(clash, same.astype(I32))
    for k in (1, 2, 4):
        clash = jnp.maximum(clash, jnp.where(within >= k, pltpu.roll(clash, k, 1), 0))
    meta = place + kind1 * 16384 + clash * (1 << 20)
    meta_ref[...] = jnp.where(lane < CAP, meta, counts)

    @pl.loop(0, OWNED // 128)
    def _(i):
        srcf[pl.ds(pl.multiple_of(i * 128, 128), 128), :] = src_ref[
            pl.ds(pl.multiple_of(i * 128, 128), 128), :
        ].astype(F32)

    @pl.loop(0, SLOTS // 128)
    def _(i):
        sendf[pl.ds(pl.multiple_of(i * 128, 128), 128), :] = jnp.zeros((128, 128), F32)

    copy.wait()

    for j in range(OWNED // 128):

        @pl.loop(0, 8)
        def _(i):
            for u in range(16):
                n = i * 16 + u
                sendf[pl.ds(slot_s[j, n], 1), :] = srcf[pl.ds(j * 128 + n, 1), :]

    @pl.loop(0, SLOTS // 128)
    def _(i):
        rows = pl.ds(pl.multiple_of(i * 128, 128), 128)
        send_ref[rows, :] = sendf[rows, :].astype(BF16)


def partners():
    tx, ty = lax.axis_index("tx"), lax.axis_index("ty")

    def to(k):
        return (tx + k % NX_DEV) % NX_DEV, (ty + k // NX_DEV) % NY_DEV

    def back(k):
        return (tx + NX_DEV - k % NX_DEV) % NX_DEV, (ty + NY_DEV - k // NX_DEV) % NY_DEV

    return tx, ty, to, back


def greet_all(to):
    barrier = pltpu.get_barrier_semaphore()

    @pl.loop(1, DEV)
    def _(k):
        pl.semaphore_signal(barrier, inc=1, device_id=to(k), device_id_type=MESH)

    return barrier


def forward_kernel(
    send_ref, msend_ref, spread_ref,
    seed_ref, idx_ref, meta_ref,
    recv, mid, mid2, last, kcol,
    ssem, rsem, xs, xr, ys, yr, lsem,
):
    tx, ty, to, back = partners()
    me_t, me_q = tx * NY_DEV + ty, ty * NX_DEV + tx
    barrier = greet_all(to)
    own = pltpu.make_async_copy(send_ref.at[me_t], recv.at[me_q], lsem.at[0])
    own.start()
    own_mid = pltpu.make_async_copy(msend_ref.at[tx], mid.at[tx], lsem.at[1])
    own_mid.start()
    pl.semaphore_wait(barrier, DEV - 1)

    def x_copy(i, peer, there):
        return pltpu.make_async_remote_copy(
            src_ref=msend_ref.at[peer], dst_ref=mid.at[there], send_sem=xs.at[i],
            recv_sem=xr.at[i], device_id=(peer, ty), device_id_type=MESH,
        )

    def y_copy(i, peer, there):
        return pltpu.make_async_remote_copy(
            src_ref=mid2.at[peer], dst_ref=last.at[there], send_sem=ys.at[i],
            recv_sem=yr.at[i], device_id=(tx, peer), device_id_type=MESH,
        )

    def d_copy(k, peer, there):
        return pltpu.make_async_remote_copy(
            src_ref=send_ref.at[peer[0] * NY_DEV + peer[1]], dst_ref=recv.at[there],
            send_sem=ssem.at[k], recv_sem=rsem.at[k], device_id=peer, device_id_type=MESH,
        )

    @pl.loop(1, NX_DEV)
    def _(i):
        x_copy(i, (tx + i) % NX_DEV, tx).start()

    @pl.loop(1, 48)
    def _(k):
        d_copy(k, to(k), me_q).start()

    own_mid.wait()

    @pl.loop(1, NX_DEV)
    def _(i):
        x_copy(i, (tx + NX_DEV - i) % NX_DEV, (tx + NX_DEV - i) % NX_DEV).wait()

    for j in range(NY_DEV):
        mid2[j] = mid[:, j, :]
    own_meta = pltpu.make_async_copy(mid2.at[ty], last.at[ty], lsem.at[2])
    own_meta.start()

    @pl.loop(1, NY_DEV)
    def _(i):
        y_copy(i, (ty + i) % NY_DEV, ty).start()

    @pl.loop(48, DEV)
    def _(k):
        d_copy(k, to(k), me_q).start()

    own_meta.wait()
    own.wait()

    @pl.loop(1, NY_DEV)
    def _(i):
        y_copy(i, (ty + NY_DEV - i) % NY_DEV, (ty + NY_DEV - i) % NY_DEV).wait()

    meta = last[...].reshape(DEV, 128)
    meta_ref[...] = meta
    idx_ref[...] = meta & 16383
    kind1 = jnp.transpose(((meta >> 14) & 31).astype(F32))[:CAP, :]
    kcol[...] = kind1

    @pl.loop(0, NY_DEV)
    def _(g):
        @pl.loop(0, NX_DEV)
        def _(i):
            k = g * NX_DEV + i

            @pl.when(k > 0)
            def _():
                a, b = back(k)
                d_copy(k, (a, b), b * NX_DEV + a).wait()

        q = (ty + NY_DEV - g) % NY_DEV
        kinds = pltpu.roll(kcol[...], (DEV - q * NX_DEV) % DEV, 1)
        kb = jnp.concatenate(
            [jnp.broadcast_to(kinds[:, i : i + 1], (CAP, 128)) for i in range(NX_DEV)], axis=0
        ).astype(BF16)
        x = recv[pl.ds(q * NX_DEV, NX_DEV)].reshape(NX_DEV * CAP, 128)
        zero = jnp.zeros_like(x)
        masked = jnp.concatenate(
            [jnp.where(kb == jnp.asarray(k + 1, BF16), x, zero) for k in range(KINDS)], axis=1
        )
        rows = pl.ds(pl.multiple_of(q * (NX_DEV * CAP), NX_DEV * CAP), NX_DEV * CAP)
        seed_ref[rows, :] = dot(masked, spread_ref[...])


def scatter_kernel(idx_s, meta_s, seed_ref, cot_ref, rhs_ref, sem):
    def load(n):
        c, l = n // NZ, n % NZ
        return pltpu.make_async_copy(
            cot_ref.at[l, :, pl.ds(pl.multiple_of(c * 128, 128), 128)],
            rhs_ref.at[pl.ds(pl.multiple_of(n * CX, CX), CX), :],
            sem.at[n],
        )

    @pl.loop(0, CH * NZ)
    def _(n):
        load(n).start()

    rhs_ref[pl.ds(PATCHES, CAP), :] = jnp.zeros((CAP, 128), F32)

    @pl.loop(0, CH * NZ)
    def _(n):
        load(n).wait()

    @pl.loop(0, DEV)
    def _(q):
        count = meta_s[q, CAP]
        for g in range(CAP // GROUP):

            @pl.when(count > g * GROUP)
            def _():
                base = pl.multiple_of(q * CAP + g * GROUP, GROUP)
                at = [pl.ds(idx_s[q, g * GROUP + u], 1) for u in range(GROUP)]
                clash = meta_s[q, g * GROUP + GROUP - 1] >> 20

                @pl.when(clash == 0)
                def _():
                    new = [rhs_ref[at[u], :] + seed_ref[pl.ds(base + u, 1), :] for u in range(GROUP)]
                    for u in range(GROUP):
                        rhs_ref[at[u], :] = new[u]

                @pl.when(clash != 0)
                def _():
                    for u in range(GROUP):
                        rhs_ref[at[u], :] = rhs_ref[at[u], :] + seed_ref[pl.ds(base + u, 1), :]


def backward_kernel(
    idx_s, slot_s, rhs_ref, cond_ref, diag_ref, kb_ref, spread_ref, deriv_ref,
    out_ref, grad_ref,
    cond, inv, g0, g1, adj, heat, hsend, recv, recvf, pulled,
    xe, ye, xh, yh,
    ssem, rsem, hs, hr, fsem, osem, lsem,
):
    tx, ty, to, back = partners()
    me_t, me_q = tx * NY_DEV + ty, ty * NX_DEV + tx
    lane = iota((8, 128), 1)

    def plane(field, buffer, n, s):
        c, l = n // NZ, n % NZ
        return (
            field.at[l, :, pl.ds(pl.multiple_of(c * 128, 128), 128)],
            buffer.at[pl.ds(pl.multiple_of(n * CX, CX), CX), :],
            s,
        )

    def load(n, which):
        return pltpu.make_async_copy(
            *plane((cond_ref, diag_ref)[which], (cond, inv)[which], n, fsem.at[which, n])
        )

    def save(n):
        hbm, vmem, s = plane(out_ref, adj, n, osem.at[n])
        return pltpu.make_async_copy(vmem, hbm, s)

    @pl.loop(0, CH * NZ)
    def _(n):
        load(n, 0).start()
        load(n, 1).start()

    barrier = greet_all(to)
    adj[pl.ds(PATCHES, CAP), :] = jnp.zeros((CAP, 128), F32)
    for g in (g0, g1):
        for c in range(CH):
            for l in (0, NZ + 1):

                @pl.loop(0, SEG // 16)
                def _(i):
                    g[pl.ds((c * (NZ + 2) + l) * SEG + i * 16, 16), :] = jnp.zeros((16, 128), F32)

    @pl.loop(0, CH * NZ)
    def _(n):
        load(n, 0).wait()
        load(n, 1).wait()

    def row_of(c, l, r):
        return pl.multiple_of(c * (NZ * CX) + l * CX + r, 8)

    def grow_of(c, l, r):
        return pl.multiple_of((c * (NZ + 2) + l + 1) * SEG + 8 + r, 8)

    def edges(acc, lo, hi, j):
        left, right = acc
        left = jnp.where(lane == j, pltpu.roll(lo, j, 1), left)
        right = jnp.where(lane == j, pltpu.roll(hi, (j + 1) % 128, 1), right)
        return left, right

    def visit(body, after=None):
        for h in range(2):

            def step(i, acc):
                for u in range(2):
                    j = i * 2 + u
                    lo, hi = body(h * 4 + j // 32, (j % 32) * 8, j, h)
                    if after is not None:
                        acc = edges(acc, lo, hi, j)
                return acc

            acc = lax.fori_loop(0, 64, step, (jnp.zeros((8, 128), F32),) * 2)
            if after is not None:
                after(h, acc)

    def keep_edges(s):
        def after(h, acc):
            ye[s, 0, pl.ds(h * 8, 8), :] = acc[0]
            ye[s, 1, pl.ds(h * 8, 8), :] = acc[1]

        return after

    def start(l, r, j, h):
        ends = []
        for c in range(CH):
            at = pl.ds(row_of(c, l, r), 8)
            q = 1.0 / inv[at, :]
            inv[at, :] = q
            g = cond[at, :] * (rhs_ref[at, :] * q)
            g0[pl.ds(grow_of(c, l, r), 8), :] = g
            ends.append(g)
        return ends[0], ends[-1]

    def sums(g, s, l, r, j, h):
        own = [g[pl.ds(grow_of(c, l, r), 8), :] for c in range(CH)]
        before = pltpu.roll(yh[s, 0, pl.ds(h * 8, 8), :], 127 - j, 1)
        behind = pltpu.roll(yh[s, 1, pl.ds(h * 8, 8), :], (128 - j) % 128, 1)
        wide = [before, *own, behind]
        out = []
        for c in range(CH):
            b = grow_of(c, l, r)
            west = pltpu.roll(jnp.where(lane == 127, wide[c], own[c]), 1, 1)
            east = pltpu.roll(jnp.where(lane == 0, wide[c + 2], own[c]), 127, 1)
            total = g[pl.ds(b - 1, 8), :] + g[pl.ds(b + 1, 8), :]
            total = total + west + east
            out.append(total + g[pl.ds(b - SEG, 8), :] + g[pl.ds(b + SEG, 8), :])
        return out

    def first(l, r, j, h):
        ends = []
        for c, total in enumerate(sums(g0, 0, l, r, j, h)):
            at = pl.ds(row_of(c, l, r), 8)
            g = cond[at, :] * ((rhs_ref[at, :] + total) * inv[at, :])
            g1[pl.ds(grow_of(c, l, r), 8), :] = g
            ends.append(g)
        return ends[0], ends[-1]

    def second(l, r, j, h):
        for c, total in enumerate(sums(g1, 1, l, r, j, h)):
            at = pl.ds(row_of(c, l, r), 8)
            adj[at, :] = (rhs_ref[at, :] + total) * inv[at, :]
        return None, None

    up, down = (tx + NX_DEV - 1) % NX_DEV, (tx + 1) % NX_DEV
    west, east = (ty + NY_DEV - 1) % NY_DEV, (ty + 1) % NY_DEV

    def halo(s, g):
        for c in range(CH):
            for l in range(NZ):
                n = c * NZ + l
                b = (c * (NZ + 2) + l + 1) * SEG + 8
                xe[s, 0, n : n + 1, :] = g[b : b + 1, :]
                xe[s, 1, n : n + 1, :] = g[b + CX - 1 : b + CX, :]
        if s == 0:
            pl.semaphore_wait(barrier, DEV - 1)
        copies = []
        for i, (src, dst, dev) in enumerate(
            (
                (ye.at[s, 0], yh.at[s, 1], (tx, west)),
                (ye.at[s, 1], yh.at[s, 0], (tx, east)),
                (xe.at[s, 0], xh.at[s, 1], (up, ty)),
                (xe.at[s, 1], xh.at[s, 0], (down, ty)),
            )
        ):
            copies.append(
                pltpu.make_async_remote_copy(
                    src_ref=src, dst_ref=dst, send_sem=hs.at[s, i], recv_sem=hr.at[s, i],
                    device_id=dev, device_id_type=MESH,
                )
            )
            copies[-1].start()
        for copy in copies:
            copy.wait()
        outer = jnp.where(tx == 0, 0.0, xh[s, 0])
        outer2 = jnp.where(tx == NX_DEV - 1, 0.0, xh[s, 1])
        for c in range(CH):
            for l in range(NZ):
                n = c * NZ + l
                b = (c * (NZ + 2) + l + 1) * SEG + 8
                g[b - 1 : b, :] = outer[n : n + 1, :]
                g[b + CX : b + CX + 1, :] = outer2[n : n + 1, :]
        yh[s, 0] = jnp.where(ty == 0, 0.0, yh[s, 0])
        yh[s, 1] = jnp.where(ty == NY_DEV - 1, 0.0, yh[s, 1])

    visit(start, keep_edges(0))
    halo(0, g0)
    visit(first, keep_edges(1))
    halo(1, g1)
    visit(second)

    @pl.loop(0, CH * NZ)
    def _(n):
        save(n).start()

    def take(q):
        for u in range(CAP):
            heat[pl.ds(u, 1), :] = adj[pl.ds(idx_s[q, u], 1), :]
        hsend[q] = heat[...].astype(BF16)

    def d_copy(k, peer, there):
        return pltpu.make_async_remote_copy(
            src_ref=hsend.at[peer[1] * NX_DEV + peer[0]], dst_ref=recv.at[there],
            send_sem=ssem.at[k], recv_sem=rsem.at[k], device_id=peer, device_id_type=MESH,
        )

    @pl.loop(1, DEV)
    def _(k):
        a, b = to(k)
        take(b * NX_DEV + a)
        d_copy(k, (a, b), me_t).start()

    take(me_q)
    own = pltpu.make_async_copy(hsend.at[me_q], recv.at[me_t], lsem)
    own.start()

    @pl.loop(0, CH * NZ)
    def _(n):
        save(n).wait()

    own.wait()

    @pl.loop(1, DEV)
    def _(k):
        a, b = back(k)
        d_copy(k, (a, b), a * NY_DEV + b).wait()

    @pl.loop(0, DEV // 4)
    def _(i):
        recvf[pl.ds(pl.multiple_of(i * 128, 128), 128), :] = (
            recv[pl.ds(i * 4, 4)].reshape(128, 128).astype(F32)
        )

    @pl.loop(0, 8)
    def _(i):
        for j in range(2):

            @pl.loop(0, 8)
            def _(v):
                for u in range(16):
                    n = v * 16 + u
                    pulled[pl.ds(j * 128 + n, 1), :] = recvf[pl.ds(slot_s[i * 2 + j, n], 1), :]

        rows = pl.ds(pl.multiple_of(i * 256, 256), 256)
        x = pulled[...].astype(BF16)
        kb = kb_ref[rows, :]
        zero = jnp.zeros_like(x)
        masked = jnp.concatenate(
            [jnp.where(kb == jnp.asarray(k, BF16), x, zero) for k in range(KINDS)], axis=1
        )
        grad_ref[rows, :] = deriv_ref[rows, :] * dot(masked, spread_ref[...])


def local(cot_field, conductance, diagonal, source_adjoint, spreading, heat_deriv, block_tile, block_patch, block_kind):
    grid16 = (OWNED // 128, 128)
    shape = jax.ShapeDtypeStruct
    send, meta, slots, kinds = pl.pallas_call(
        route_kernel,
        out_shape=(
            shape((SLOTS, 128), BF16),
            shape((DEV, 128), I32),
            shape(grid16, I32),
            shape((OWNED, 128), BF16),
        ),
        in_specs=[VMEM] * 4,
        out_specs=(VMEM,) * 4,
        scratch_shapes=[
            pltpu.VMEM((OWNED, 128), F32),
            pltpu.VMEM((SLOTS, 128), F32),
            pltpu.SMEM(grid16, I32),
            pltpu.SemaphoreType.DMA,
        ],
        compiler_params=pltpu.CompilerParams(vmem_limit_bytes=20 << 20),
        name="route",
    )(block_tile.reshape(grid16), block_patch.reshape(grid16), block_kind.reshape(grid16), source_adjoint)

    dma = pltpu.SemaphoreType.DMA
    seeds, idx, got = pl.pallas_call(
        forward_kernel,
        out_shape=(shape((SLOTS, 128), F32), shape((DEV, 128), I32), shape((DEV, 128), I32)),
        in_specs=[VMEM] * 3,
        out_specs=(VMEM,) * 3,
        scratch_shapes=[
            pltpu.VMEM((DEV, CAP, 128), BF16),
            pltpu.VMEM((NX_DEV, NY_DEV, 128), I32),
            pltpu.VMEM((NY_DEV, NX_DEV, 128), I32),
            pltpu.VMEM((NY_DEV, NX_DEV, 128), I32),
            pltpu.VMEM((CAP, DEV), F32),
            dma((DEV,)),
            dma((DEV,)),
            dma((NX_DEV,)),
            dma((NX_DEV,)),
            dma((NY_DEV,)),
            dma((NY_DEV,)),
            dma((3,)),
        ],
        compiler_params=pltpu.CompilerParams(
            collective_id=0, has_side_effects=True, vmem_limit_bytes=24 << 20
        ),
        name="forward",
    )(
        send.reshape(DEV, CAP, 128),
        meta.reshape(NX_DEV, NY_DEV, 128),
        spreading.reshape(KINDS * 128, 128),
    )

    rhs = pl.pallas_call(
        scatter_kernel,
        out_shape=shape((ROWS, 128), F32),
        in_specs=[SMEM, SMEM, VMEM, ANY],
        out_specs=VMEM,
        scratch_shapes=[dma((CH * NZ,))],
        compiler_params=pltpu.CompilerParams(vmem_limit_bytes=24 << 20),
        name="scatter",
    )(idx, got, seeds, cot_field)

    spread_t = jnp.swapaxes(spreading, 1, 2).reshape(KINDS * 128, 128)
    flat = pltpu.VMEM((PATCHES, 128), F32)
    padded = pltpu.VMEM((GROWS, 128), F32)
    temp, grad = pl.pallas_call(
        backward_kernel,
        out_shape=(shape(cot_field.shape, F32), shape((OWNED, 128), F32)),
        in_specs=[SMEM, SMEM, VMEM, ANY, ANY, VMEM, VMEM, VMEM],
        out_specs=(ANY, VMEM),
        scratch_shapes=[
            flat,
            flat,
            padded,
            padded,
            pltpu.VMEM((ROWS, 128), F32),
            pltpu.VMEM((CAP, 128), F32),
            pltpu.VMEM((DEV, CAP, 128), BF16),
            pltpu.VMEM((DEV, CAP, 128), BF16),
            pltpu.VMEM((SLOTS, 128), F32),
            pltpu.VMEM((256, 128), F32),
            pltpu.VMEM((2, 2, CH * NZ, 128), F32),
            pltpu.VMEM((2, 2, 16, 128), F32),
            pltpu.VMEM((2, 2, CH * NZ, 128), F32),
            pltpu.VMEM((2, 2, 16, 128), F32),
            dma((DEV,)),
            dma((DEV,)),
            dma((2, 4)),
            dma((2, 4)),
            dma((2, CH * NZ)),
            dma((CH * NZ,)),
            dma,
        ],
        compiler_params=pltpu.CompilerParams(
            collective_id=1, has_side_effects=True, vmem_limit_bytes=58 << 20
        ),
        name="backward",
    )(idx, slots, rhs, conductance, diagonal, kinds, spread_t, heat_deriv)
    return temp, grad


def solution(mesh):
    blocks = P(("tx", "ty"))
    field = P(None, "tx", "ty")
    in_specs = (
        field, field, field, P(("tx", "ty"), None), P(), P(("tx", "ty"), None),
        P(("tx", "ty"), None), blocks, blocks,
    )
    out_specs = (field, P(("tx", "ty"), None))
    return jax.shard_map(local, mesh=mesh, in_specs=in_specs, out_specs=out_specs, check_vma=False)
```

time: 242 us -> 186 us (0.77)
  Pallas kernels: 0 us -> 167 us
  other arithmetic: 67.4 us -> 0 us
  starting transfers between devices: 53.6 us -> 0 us
  waiting for transfers between devices: 51.4 us -> 0 us
  local copies, waits for them, and re-layouts: 57.6 us -> 17.4 us
  matrix products: 9.78 us -> 0 us
    pallas_call x0 -> x4, Pallas kernels: none -> 167 us  [the longest x1 103 us: local(): pl.pallas_call(backward_kernel, out_shape=(shape(cot_field.shape, F32), s...]
    all_to_all x3 -> x0, waiting for transfers between devices: 41.9 us -> none  [the longest x1 23.1 us: local(): lax.all_to_all(send_values.reshape(devices, capacity, 128), ('tx', 'ty'),...]
    mul x4 -> x0, other arithmetic: 38.8 us -> none  [the longest x2 22.2 us: local(): padded = padded_2(conductance * adjoint, (('tx', 1), ('ty', 2)), 1)]
    all_to_all x3 -> x0, starting transfers between devices: 33.3 us -> none  [the longest x1 12 us: local(): lax.all_to_all(heat_rows.reshape(devices, capacity, 128), ('tx', 'ty'), s...]
    scatter-add x1 -> x0, other arithmetic: 24.3 us -> none  [local(): cot_field.reshape(patches, 128).at[got_ids].add(got_values, mode='drop')]
    gather x2 -> x0, local copies, waits for them, and re-layouts: 21.2 us -> none  [the longest x1 15 us: local(): jnp.take(adjoint.reshape(patches, 128), got_ids, axis=0, mode='clip')]
    ppermute x8 -> x0, starting transfers between devices: 20.3 us -> none  [the longest x4 13.8 us: padded_2(): before = lax.ppermute(last, axis, up)]
    scatter x2 -> x0, local copies, waits for them, and re-layouts: 15.2 us -> none  [the longest x1 8.23 us: local(): jnp.full((slots,), patches, jnp.int32).at[slot_index].set(block_patch)]
  transfers between devices with their start and end apart: 11 -> 0, of which waited for: 6 -> 0; matrix products, arithmetic and copies ran while one was open for 8% -> 0% of each run, Pallas kernels for 0% -> 0%
where the time goes in v1:
time: 186 us
  Pallas kernels  167 us (90%)
  local copies, waits for them, and re-layouts  17.4 us (9%)
    pallas_call x1, Pallas kernels, local(): pl.pallas_call(backward_kernel, out_shape=(shape(cot_field.shape, F32), s...  103 us
    pallas_call x1, Pallas kernels, local(): pl.pallas_call(forward_kernel, out_shape=(shape((SLOTS, 128), F32), shape...  39.5 us
    pallas_call x1, Pallas kernels, local(): pl.pallas_call(scatter_kernel, out_shape=shape((ROWS, 128), F32), in_spec...  18.3 us
    unnamed x24, local copies, waits for them, and re-layouts  15.4 us
    pallas_call x1, Pallas kernels, local(): pl.pallas_call(route_kernel, out_shape=(shape((SLOTS, 128), BF16), shape(...  6.98 us

profile of v1, /device:TPU:1, one launch (start us, length us, event | category | flops | bytes accessed | tf_op | source)
XLA Modules:
  0.0 185.6 jit_solution(11871675990506398268)
XLA Ops:
  0.6 2.0 %copy.11 = bf16[16,128,128]{2,1,0:T(8,128)(2,1)} copy(bf16[16,128,128]{1,2,0:T(8,128)(2,1)} %bitcast.8) | data formatting | bytes 1048576 | tf_op jit(solution)/shard_map/transpose | solution.py:573
  2.7 0.0 copy-start.4
  2.7 1.0 copy-done.4
  3.7 0.7 copy-done.6
  4.4 0.7 copy-done.7
  5.1 0.7 copy-done.8
  5.8 7.0 %route.1 = (bf16[4096,128]{1,0:T(8,128)(2,1)S(1)}, s32[128,128]{1,0:T(8,128)S(1)}, s32[16,128]{1,0:T(8,128)S(1)}, bf16[2048,128]{1,0:T(8,128)(2,1)S(1)}) custom-call(s32[16,128]{1,0:T(8,128)S(1)} %bitcast.12, s32[16,128]{1,0:T(8,128)S(1)} %bitcast.13, s32[16,128]{1,0:T(8,128)S(1)} %bitcast.14, bf16[2048,128]{1,0:T(8,128)(2,1)S(1)} %copy-done.4), custom_call_target="tpu_custom_call" | custom-call | tf_op jit(solution)/shard_map/route/pallas_call | solution.py:513
  12.8 0.0 copy-start.3
  12.8 0.8 copy-done.3
  13.6 0.6 copy-done.9
  14.2 1.0 copy-done.2
  15.2 39.5 %forward.1 = (f32[4096,128]{1,0:T(8,128)S(1)}, s32[128,128]{1,0:T(8,128)S(1)}, s32[128,128]{1,0:T(8,128)S(1)}) custom-call(bf16[128,32,128]{2,1,0:T(8,128)(2,1)S(1)} %bitcast.10, s32[8,16,128]{2,1,0:T(8,128)S(1)} %bitcast.11, bf16[2048,128]{1,0:T(8,128)(2,1)S(1)} %bitcast.9), custom_call_target="tpu_custom_call" | custom-call | tf_op jit(solution)/shard_map/forward/pallas_call | solution.py:534
  54.7 0.0 copy-start.5
  54.7 0.0 copy-start.1
  54.7 2.2 %copy-done.1 = f32[8,256,512]{2,1,0:T(8,128)S(1)} copy-done((f32[8,256,512]{2,1,0:T(8,128)S(1)}, f32[8,256,512]{2,1,0:T(8,128)}, u32[]{:S(2)}) %copy-start.1) | copy-done | bytes 4194328
  56.9 18.3 %scatter.1.rhs_ref = f32[8224,128]{1,0:T(8,128)S(1)} custom-call(s32[128,128]{1,0:T(8,128)S(1)} %get-tuple-element.11.idx_s, s32[128,128]{1,0:T(8,128)S(1)} %get-tuple-element.13.meta_s, f32[4096,128]{1,0:T(8,128)S(1)} %get-tuple-element.14.seed_ref, f32[8,256,512]{2,1,0:T(8,128)S(1)} %copy-done.1), custom_call_target="tpu_custom_call" | custom-call | tf_op jit(solution)/shard_map/scatter/pallas_call | solution.py:563
  75.3 0.0 copy-done.5
  75.3 0.0 copy-start
  75.3 1.9 %copy-done = f32[8224,128]{1,0:T(8,128)} copy-done((f32[8224,128]{1,0:T(8,128)}, f32[8224,128]{1,0:T(8,128)S(1)}, u32[]{:S(2)}) %copy-start) | copy-done | bytes 4210712
  77.2 102.7 %backward.1 = (f32[8,256,512]{2,1,0:T(8,128)}, f32[2048,128]{1,0:T(8,128)}) custom-call(s32[128,128]{1,0:T(8,128)} %copy-done.5, s32[16,128]{1,0:T(8,128)} %copy-done.9, f32[8224,128]{1,0:T(8,128)} %copy-done, f32[8,256,512]{2,1,0:T(8,128)} %cond_ref.1, f32[8,256,512]{2,1,0:T(8,128)} %diag_ref.1, bf16[2048,128]{1,0:T(8,128)(2,1)} %copy-done.3, ...), custom_call_target="tpu_custom_call" | custom-call | tf_op jit(solution)/shard_map/backward/pallas_call | solution.py:576
  179.9 0.0 copy-start.10
  179.9 4.7 %copy.14 = f32[8,256,512]{2,1,0:T(8,128)} copy(f32[8,256,512]{2,1,0:T(8,128)} %get-tuple-element.18) | data formatting | bytes 8388608
  184.7 0.0 copy-done.10
  184.7 1.0 copy.15
  (5 shorter events, 0.0 us)
Async XLA Ops:
  2.7 1.0 copy-start.4
  3.7 0.7 copy-start.6
  4.4 0.7 copy-start.7
  5.1 0.7 copy-start.8
  12.8 0.8 copy-start.3
  13.6 0.6 copy-start.9
  14.2 1.0 copy-start.2
  54.7 20.6 %copy-start.5 = (s32[128,128]{1,0:T(8,128)}, s32[128,128]{1,0:T(8,128)S(1)}, u32[]{:S(2)}) copy-start(s32[128,128]{1,0:T(8,128)S(1)} %get-tuple-element.11.idx_s) | copy-start | bytes 196612
  54.7 2.2 %copy-start.1 = (f32[8,256,512]{2,1,0:T(8,128)S(1)}, f32[8,256,512]{2,1,0:T(8,128)}, u32[]{:S(2)}) copy-start(f32[8,256,512]{2,1,0:T(8,128)} %cot_ref.1) | copy-start | bytes 12582916
  75.3 2.0 %copy-start = (f32[8224,128]{1,0:T(8,128)}, f32[8224,128]{1,0:T(8,128)S(1)}, u32[]{:S(2)}) copy-start(f32[8224,128]{1,0:T(8,128)S(1)} %scatter.1.rhs_ref) | copy-start | bytes 12632068
  179.9 4.7 %copy-start.10 = (f32[2048,128]{1,0:T(8,128)S(1)}, f32[2048,128]{1,0:T(8,128)}, u32[]{:S(2)}) copy-start(f32[2048,128]{1,0:T(8,128)} %get-tuple-element.19) | copy-start | bytes 3145732

commit v2 on v1

--- a/solution.py
+++ b/solution.py
@@ -20,6 +20,7 @@
 GROWS = CH * (NZ + 2) * SEG
 OWNED = 2048
 GROUP = 8
+UNROLL, BATCH = 16, 1
 F32, BF16, I32 = jnp.float32, jnp.bfloat16, jnp.int32
 MESH = pl.DeviceIdType.MESH
 VMEM = pl.BlockSpec(memory_space=pltpu.VMEM)
@@ -37,7 +38,7 @@
 
 
 def route_kernel(
-    tile_ref, patch_ref, kind_ref, src_ref,
+    table_ref, src_ref,
     send_ref, meta_ref, slot_ref, kb_ref,
     srcf, sendf, slot_s, sem,
 ):
@@ -48,9 +49,7 @@
     count = jnp.zeros((128, 128), F32)
     table = jnp.zeros((128, 128), F32)
     for j in range(OWNED // 128):
-        tile = tile_ref[j : j + 1, :]
-        patch = patch_ref[j : j + 1, :]
-        kind = kind_ref[j : j + 1, :]
+        tile, patch, kind = (table_ref[n * 16 + j : n * 16 + j + 1, :] for n in range(3))
         place = (patch & (CH - 1)) * (NZ * CX) + (patch >> 2)
         hit = (sub == tile).astype(F32)
         hit16 = hit.astype(BF16)
@@ -278,53 +277,28 @@
 def backward_kernel(
     idx_s, slot_s, rhs_ref, cond_ref, diag_ref, kb_ref, spread_ref, deriv_ref,
     out_ref, grad_ref,
-    cond, inv, g0, g1, adj, heat, hsend, recv, recvf, pulled,
+    inv, g0, g1, adj, heat, hsend, recv, recvf, pulled,
     xe, ye, xh, yh,
-    ssem, rsem, hs, hr, fsem, osem, lsem,
+    ssem, rsem, hs, hr, lsem,
 ):
     tx, ty, to, back = partners()
     me_t, me_q = tx * NY_DEV + ty, ty * NX_DEV + tx
     lane = iota((8, 128), 1)
-
-    def plane(field, buffer, n, s):
-        c, l = n // NZ, n % NZ
-        return (
-            field.at[l, :, pl.ds(pl.multiple_of(c * 128, 128), 128)],
-            buffer.at[pl.ds(pl.multiple_of(n * CX, CX), CX), :],
-            s,
-        )
-
-    def load(n, which):
-        return pltpu.make_async_copy(
-            *plane((cond_ref, diag_ref)[which], (cond, inv)[which], n, fsem.at[which, n])
-        )
-
-    def save(n):
-        hbm, vmem, s = plane(out_ref, adj, n, osem.at[n])
-        return pltpu.make_async_copy(vmem, hbm, s)
-
-    @pl.loop(0, CH * NZ)
-    def _(n):
-        load(n, 0).start()
-        load(n, 1).start()
-
     barrier = greet_all(to)
     adj[pl.ds(PATCHES, CAP), :] = jnp.zeros((CAP, 128), F32)
     for g in (g0, g1):
         for c in range(CH):
             for l in (0, NZ + 1):
 
-                @pl.loop(0, SEG // 16)
+                @pl.loop(0, CX // 64)
                 def _(i):
-                    g[pl.ds((c * (NZ + 2) + l) * SEG + i * 16, 16), :] = jnp.zeros((16, 128), F32)
-
-    @pl.loop(0, CH * NZ)
-    def _(n):
-        load(n, 0).wait()
-        load(n, 1).wait()
+                    g[pl.ds((c * (NZ + 2) + l) * SEG + 8 + i * 64, 64), :] = jnp.zeros((64, 128), F32)
+
+    def cell(c, l, r):
+        return l, pl.ds(r, 8), pl.ds(c * 128, 128)
 
     def row_of(c, l, r):
-        return pl.multiple_of(c * (NZ * CX) + l * CX + r, 8)
+        return pl.ds(pl.multiple_of(c * (NZ * CX) + l * CX + r, 8), 8)
 
     def grow_of(c, l, r):
         return pl.multiple_of((c * (NZ + 2) + l + 1) * SEG + 8 + r, 8)
@@ -339,14 +313,20 @@
         for h in range(2):
 
             def step(i, acc):
-                for u in range(2):
-                    j = i * 2 + u
-                    lo, hi = body(h * 4 + j // 32, (j % 32) * 8, j, h)
-                    if after is not None:
-                        acc = edges(acc, lo, hi, j)
+                for v in range(0, UNROLL, BATCH):
+                    stores = []
+                    for u in range(v, v + BATCH):
+                        j = i * UNROLL + u
+                        r = pl.multiple_of((i % (32 // UNROLL)) * (UNROLL * 8), 8) + u * 8
+                        writes, lo, hi = body(h * 4 + i // (32 // UNROLL), r, j, h)
+                        stores += writes
+                        if after is not None:
+                            acc = edges(acc, lo, hi, j)
+                    for ref, at, value in stores:
+                        ref[at] = value
                 return acc
 
-            acc = lax.fori_loop(0, 64, step, (jnp.zeros((8, 128), F32),) * 2)
+            acc = lax.fori_loop(0, 128 // UNROLL, step, (jnp.zeros((8, 128), F32),) * 2)
             if after is not None:
                 after(h, acc)
 
@@ -358,15 +338,14 @@
         return after
 
     def start(l, r, j, h):
-        ends = []
+        writes, ends = [], []
         for c in range(CH):
-            at = pl.ds(row_of(c, l, r), 8)
-            q = 1.0 / inv[at, :]
-            inv[at, :] = q
-            g = cond[at, :] * (rhs_ref[at, :] * q)
-            g0[pl.ds(grow_of(c, l, r), 8), :] = g
+            q = 1.0 / diag_ref[cell(c, l, r)]
+            g = cond_ref[cell(c, l, r)] * (rhs_ref[row_of(c, l, r), :] * q)
+            writes.append((inv, (row_of(c, l, r), slice(None)), q))
+            writes.append((g0, (pl.ds(grow_of(c, l, r), 8), slice(None)), g))
             ends.append(g)
-        return ends[0], ends[-1]
+        return writes, ends[0], ends[-1]
 
     def sums(g, s, l, r, j, h):
         own = [g[pl.ds(grow_of(c, l, r), 8), :] for c in range(CH)]
@@ -384,19 +363,22 @@
         return out
 
     def first(l, r, j, h):
-        ends = []
+        writes, ends = [], []
         for c, total in enumerate(sums(g0, 0, l, r, j, h)):
-            at = pl.ds(row_of(c, l, r), 8)
-            g = cond[at, :] * ((rhs_ref[at, :] + total) * inv[at, :])
-            g1[pl.ds(grow_of(c, l, r), 8), :] = g
+            at = row_of(c, l, r), slice(None)
+            g = cond_ref[cell(c, l, r)] * ((rhs_ref[at] + total) * inv[at])
+            writes.append((g1, (pl.ds(grow_of(c, l, r), 8), slice(None)), g))
             ends.append(g)
-        return ends[0], ends[-1]
+        return writes, ends[0], ends[-1]
 
     def second(l, r, j, h):
+        writes = []
         for c, total in enumerate(sums(g1, 1, l, r, j, h)):
-            at = pl.ds(row_of(c, l, r), 8)
-            adj[at, :] = (rhs_ref[at, :] + total) * inv[at, :]
-        return None, None
+            at = row_of(c, l, r), slice(None)
+            value = (rhs_ref[at] + total) * inv[at]
+            writes.append((adj, at, value))
+            writes.append((out_ref, cell(c, l, r), value))
+        return writes, None, None
 
     up, down = (tx + NX_DEV - 1) % NX_DEV, (tx + 1) % NX_DEV
     west, east = (ty + NY_DEV - 1) % NY_DEV, (ty + 1) % NY_DEV
@@ -445,10 +427,6 @@
     halo(1, g1)
     visit(second)
 
-    @pl.loop(0, CH * NZ)
-    def _(n):
-        save(n).start()
-
     def take(q):
         for u in range(CAP):
             heat[pl.ds(u, 1), :] = adj[pl.ds(idx_s[q, u], 1), :]
@@ -470,10 +448,6 @@
     own = pltpu.make_async_copy(hsend.at[me_q], recv.at[me_t], lsem)
     own.start()
 
-    @pl.loop(0, CH * NZ)
-    def _(n):
-        save(n).wait()
-
     own.wait()
 
     @pl.loop(1, DEV)
@@ -501,10 +475,11 @@
         x = pulled[...].astype(BF16)
         kb = kb_ref[rows, :]
         zero = jnp.zeros_like(x)
-        masked = jnp.concatenate(
-            [jnp.where(kb == jnp.asarray(k, BF16), x, zero) for k in range(KINDS)], axis=1
-        )
-        grad_ref[rows, :] = deriv_ref[rows, :] * dot(masked, spread_ref[...])
+        total = jnp.zeros((256, 128), F32)
+        for k in range(KINDS):
+            masked = jnp.where(kb == jnp.asarray(k, BF16), x, zero)
+            total = total + lax.dot_general(masked, spread_ref[k], NT, preferred_element_type=F32)
+        grad_ref[rows, :] = deriv_ref[rows, :] * total
 
 
 def local(cot_field, conductance, diagonal, source_adjoint, spreading, heat_deriv, block_tile, block_patch, block_kind):
@@ -518,7 +493,7 @@
             shape(grid16, I32),
             shape((OWNED, 128), BF16),
         ),
-        in_specs=[VMEM] * 4,
+        in_specs=[VMEM] * 2,
         out_specs=(VMEM,) * 4,
         scratch_shapes=[
             pltpu.VMEM((OWNED, 128), F32),
@@ -528,7 +503,10 @@
         ],
         compiler_params=pltpu.CompilerParams(vmem_limit_bytes=20 << 20),
         name="route",
-    )(block_tile.reshape(grid16), block_patch.reshape(grid16), block_kind.reshape(grid16), source_adjoint)
+    )(
+        jnp.concatenate([x.reshape(grid16) for x in (block_tile, block_patch, block_kind)]),
+        source_adjoint,
+    )
 
     dma = pltpu.SemaphoreType.DMA
     seeds, idx, got = pl.pallas_call(
@@ -570,16 +548,14 @@
         name="scatter",
     )(idx, got, seeds, cot_field)
 
-    spread_t = jnp.swapaxes(spreading, 1, 2).reshape(KINDS * 128, 128)
     flat = pltpu.VMEM((PATCHES, 128), F32)
     padded = pltpu.VMEM((GROWS, 128), F32)
     temp, grad = pl.pallas_call(
         backward_kernel,
         out_shape=(shape(cot_field.shape, F32), shape((OWNED, 128), F32)),
-        in_specs=[SMEM, SMEM, VMEM, ANY, ANY, VMEM, VMEM, VMEM],
-        out_specs=(ANY, VMEM),
+        in_specs=[SMEM, SMEM, VMEM, VMEM, VMEM, VMEM, VMEM, VMEM],
+        out_specs=(VMEM, VMEM),
         scratch_shapes=[
-            flat,
             flat,
             padded,
             padded,
@@ -597,15 +573,13 @@
             dma((DEV,)),
             dma((2, 4)),
             dma((2, 4)),
-            dma((2, CH * NZ)),
-            dma((CH * NZ,)),
             dma,
         ],
         compiler_params=pltpu.CompilerParams(
-            collective_id=1, has_side_effects=True, vmem_limit_bytes=58 << 20
+            collective_id=1, has_side_effects=True, vmem_limit_bytes=28 << 20
         ),
         name="backward",
-    )(idx, slots, rhs, conductance, diagonal, kinds, spread_t, heat_deriv)
+    )(idx, slots, rhs, conductance, diagonal, kinds, spreading, heat_deriv)
     return temp, grad
 
 

time: 186 us -> 133 us (0.72)
  Pallas kernels: 167 us -> 124 us
  local copies, waits for them, and re-layouts: 17.4 us -> 7.26 us
    pallas_call x1, Pallas kernels: 103 us -> 59.6 us  [local(): pl.pallas_call(backward_kernel, out_shape=(shape(cot_field.shape, F32), s...]
    unnamed x24 -> x16, local copies, waits for them, and re-layouts: 15.4 us -> 7.26 us
    transpose x1 -> x0, local copies, waits for them, and re-layouts: 2.04 us -> none  [local(): spread_t = jnp.swapaxes(spreading, 1, 2).reshape(KINDS * 128, 128)]
where the time goes in v2:
time: 133 us
  Pallas kernels  124 us (93%)
  local copies, waits for them, and re-layouts  7.26 us (5%)
    pallas_call x1, Pallas kernels, local(): pl.pallas_call(backward_kernel, out_shape=(shape(cot_field.shape, F32), s...  59.6 us
    pallas_call x1, Pallas kernels, local(): pl.pallas_call(forward_kernel, out_shape=(shape((SLOTS, 128), F32), shape...  39.5 us
    pallas_call x1, Pallas kernels, local(): pl.pallas_call(scatter_kernel, out_shape=shape((ROWS, 128), F32), in_spec...  18.1 us
    unnamed x16, local copies, waits for them, and re-layouts  7.26 us
    pallas_call x1, Pallas kernels, local(): pl.pallas_call(route_kernel, out_shape=(shape((SLOTS, 128), BF16), shape(...  6.98 us

profile of v2, /device:TPU:1, one launch (start us, length us, event | category | flops | bytes accessed | tf_op | source)
XLA Modules:
  0.0 132.8 jit_solution(7498188982622527269)
XLA Ops:
  0.6 0.7 pad_add_fusion.table_ref
  1.4 0.0 copy-start.6
  1.4 1.0 copy-done.6
  2.4 7.0 %route.1 = (bf16[4096,128]{1,0:T(8,128)(2,1)S(1)}, s32[128,128]{1,0:T(8,128)S(1)}, s32[16,128]{1,0:T(8,128)S(1)}, bf16[2048,128]{1,0:T(8,128)(2,1)S(1)}) custom-call(s32[48,128]{1,0:T(8,128)S(1)} %pad_add_fusion.table_ref, bf16[2048,128]{1,0:T(8,128)(2,1)S(1)} %copy-done.6), custom_call_target="tpu_custom_call" | custom-call | tf_op jit(solution)/shard_map/route/pallas_call | solution.py:488
  9.4 0.0 copy-start.3
  9.4 1.0 copy-done.3
  10.4 39.5 %forward.1 = (f32[4096,128]{1,0:T(8,128)S(1)}, s32[128,128]{1,0:T(8,128)S(1)}, s32[128,128]{1,0:T(8,128)S(1)}) custom-call(bf16[128,32,128]{2,1,0:T(8,128)(2,1)S(1)} %bitcast.7, s32[8,16,128]{2,1,0:T(8,128)S(1)} %bitcast.8, bf16[2048,128]{1,0:T(8,128)(2,1)S(1)} %bitcast.6), custom_call_target="tpu_custom_call" | custom-call | tf_op jit(solution)/shard_map/forward/pallas_call | solution.py:512
  49.9 0.0 copy-start
  49.9 2.2 %copy-done = f32[8,256,512]{2,1,0:T(8,128)S(1)} copy-done((f32[8,256,512]{2,1,0:T(8,128)S(1)}, f32[8,256,512]{2,1,0:T(8,128)}, u32[]{:S(2)}) %copy-start) | copy-done | bytes 4194328
  52.1 0.0 copy-start.1
  52.1 0.0 copy-start.2
  52.1 0.0 copy-start.4
  52.1 0.0 copy-start.5
  52.1 18.1 %scatter.1.rhs_ref = f32[8224,128]{1,0:T(8,128)S(1)} custom-call(s32[128,128]{1,0:T(8,128)S(1)} %get-tuple-element.11.idx_s, s32[128,128]{1,0:T(8,128)S(1)} %get-tuple-element.13.meta_s, f32[4096,128]{1,0:T(8,128)S(1)} %get-tuple-element.14.seed_ref, f32[8,256,512]{2,1,0:T(8,128)S(1)} %copy-done), custom_call_target="tpu_custom_call" | custom-call | tf_op jit(solution)/shard_map/scatter/pallas_call | solution.py:541
  70.2 0.0 copy-done.1
  70.2 0.0 copy-done.2
  70.3 0.0 copy-done.4
  70.3 0.0 copy-done.5
  70.3 59.6 %backward.1 = (f32[8,256,512]{2,1,0:T(8,128)S(1)}, f32[2048,128]{1,0:T(8,128)S(1)}) custom-call(s32[128,128]{1,0:T(8,128)S(1)} %get-tuple-element.11.idx_s, s32[16,128]{1,0:T(8,128)S(1)} %get-tuple-element.12.slot_s, f32[8224,128]{1,0:T(8,128)S(1)} %scatter.1.rhs_ref, f32[8,256,512]{2,1,0:T(8,128)S(1)} %copy-done.1, f32[8,256,512]{2,1,0:T(8,128)S(1)} %copy-done.2, ...), custom_call_target="tpu_custom_call" | custom-call | tf_op jit(solution)/shard_map/backward/pallas_call | solution.py:553
  129.8 2.0 %copy.13 = f32[8,256,512]{2,1,0:T(8,128)} copy(f32[8,256,512]{2,1,0:T(8,128)S(1)} %get-tuple-element.18) | data formatting | bytes 8388608
  131.9 1.0 copy.14
Async XLA Ops:
  1.4 1.0 copy-start.6
  9.4 1.0 copy-start.3
  49.9 2.2 %copy-start = (f32[8,256,512]{2,1,0:T(8,128)S(1)}, f32[8,256,512]{2,1,0:T(8,128)}, u32[]{:S(2)}) copy-start(f32[8,256,512]{2,1,0:T(8,128)} %cot_ref.1) | copy-start | bytes 12582916
  52.1 18.1 %copy-start.1 = (f32[8,256,512]{2,1,0:T(8,128)S(1)}, f32[8,256,512]{2,1,0:T(8,128)}, u32[]{:S(2)}) copy-start(f32[8,256,512]{2,1,0:T(8,128)} %cond_ref.1) | copy-start | bytes 12582916
  52.1 18.1 %copy-start.2 = (f32[8,256,512]{2,1,0:T(8,128)S(1)}, f32[8,256,512]{2,1,0:T(8,128)}, u32[]{:S(2)}) copy-start(f32[8,256,512]{2,1,0:T(8,128)} %diag_ref.1) | copy-start | bytes 12582916
  52.1 18.1 %copy-start.4 = (bf16[16,128,128]{2,1,0:T(8,128)(2,1)S(1)}, bf16[16,128,128]{2,1,0:T(8,128)(2,1)}, u32[]{:S(2)}) copy-start(bf16[16,128,128]{2,1,0:T(8,128)(2,1)} %spread_ref.1) | copy-start | bytes 1572868
  52.1 18.2 %copy-start.5 = (f32[2048,128]{1,0:T(8,128)S(1)}, f32[2048,128]{1,0:T(8,128)}, u32[]{:S(2)}) copy-start(f32[2048,128]{1,0:T(8,128)} %deriv_ref.1) | copy-start | bytes 3145732

commit v3 on v2

v3 whole, which is shorter than its diff:
```python
import functools

import jax
import jax.numpy as jnp
from jax import lax
from jax.experimental import pallas as pl
from jax.experimental.pallas import tpu as pltpu
from jax.sharding import PartitionSpec as P

NX_DEV, NY_DEV = 8, 16
DEV = NX_DEV * NY_DEV
CAP = 32
SLOTS = DEV * CAP
KINDS = 16
NZ, CX, CY = 8, 256, 512
CH = CY // 128
PATCHES = NZ * CX * CH
ROWS = PATCHES + CAP
SEG = CX + 16
GROWS = CH * (NZ + 2) * SEG
OWNED = 2048
GROUP = 8
AHEAD = 6
UNROLL, BATCH = 16, 1
F32, BF16, I32 = jnp.float32, jnp.bfloat16, jnp.int32
MESH = pl.DeviceIdType.MESH
VMEM = pl.BlockSpec(memory_space=pltpu.VMEM)
SMEM = pl.BlockSpec(memory_space=pltpu.SMEM)
ANY = pl.BlockSpec(memory_space=pl.ANY)
NT = (((1,), (1,)), ((), ()))


def dot(a, b):
    return jnp.dot(a, b, preferred_element_type=F32)


def iota(shape, dim):
    return lax.broadcasted_iota(I32, shape, dim)


def route(table_ref, slot_ref, kb_ref):
    sub, lane = iota((128, 128), 0), iota((128, 128), 1)
    before = (sub < lane).astype(F32).astype(BF16)
    ones = jnp.ones((128, 128), BF16)
    rank_row = iota((CAP, 128), 0)
    count = jnp.zeros((128, 128), F32)
    held = jnp.zeros((128, 128), F32)
    block = jnp.zeros((CAP, 128), F32)
    for j in range(OWNED // 128):
        tile, patch, kind = (table_ref[n * 16 + j : n * 16 + j + 1, :] for n in range(3))
        place = (patch & (CH - 1)) * (NZ * CX) + (patch >> 2)
        hit = (sub == tile).astype(F32)
        hit16 = hit.astype(BF16)
        rank = jnp.sum(hit * (dot(hit16, before) + count), axis=0, keepdims=True).astype(I32)
        count = count + dot(hit16, ones)
        slot_ref[j : j + 1, :] = tile * CAP + rank
        at = (rank_row == rank).astype(F32)
        parts = jnp.concatenate(
            [
                at * (place >> 7).astype(F32),
                at * (place & 127).astype(F32),
                at * (kind + 1).astype(F32),
                jnp.zeros((128 - 3 * CAP, 128), F32),
            ],
            axis=0,
        ).astype(BF16)
        held = held + lax.dot_general(hit16, parts, NT, preferred_element_type=F32)
        numbers = jnp.concatenate([at * iota((1, 128), 1).astype(F32), at], axis=0).astype(BF16)
        found = lax.dot_general(numbers, hit16, NT, preferred_element_type=F32)
        block = block + found[:CAP] + found[CAP:] * (128.0 * j)
        kb_ref[pl.ds(j * 128, 128), :] = jnp.transpose(
            jnp.broadcast_to(kind.astype(F32), (128, 128))
        ).astype(BF16)
    counts = count.astype(I32)
    place = (held * 128.0 + pltpu.roll(held, 128 - CAP, 1)).astype(I32)
    kind1 = pltpu.roll(held, 128 - 2 * CAP, 1).astype(I32)
    place = jnp.where(lane < counts, place, PATCHES + lane)
    within = lane & (GROUP - 1)
    clash = jnp.zeros((128, 128), I32)
    for k in range(1, GROUP):
        same = (pltpu.roll(place, k, 1) == place) & (within >= k)
        clash = jnp.maximum(clash, same.astype(I32))
    for k in (1, 2, 4, 8):
        if k < GROUP:
            clash = jnp.maximum(clash, jnp.where(within >= k, pltpu.roll(clash, k, 1), 0))
    meta = place + kind1 * 16384 + clash * (1 << 20)
    return jnp.where(lane < CAP, meta, counts), block.astype(I32) & (OWNED - 1)


def partners():
    tx, ty = lax.axis_index("tx"), lax.axis_index("ty")

    def to(g, i):
        return lax.rem(tx + i, NX_DEV), lax.rem(ty + g * 5, NY_DEV)

    def from_y(g):
        return lax.rem(ty + 5 * NY_DEV - g * 5, NY_DEV)

    return tx, ty, to, from_y


def each(do, lo=0, hi=NY_DEV):
    if lo == 0:
        for i in range(1, NX_DEV):
            do(0, i)

    @pl.loop(max(lo, 1), hi)
    def _(g):
        for i in range(NX_DEV):
            do(g, i)


def greet_all(to):
    barrier = pltpu.get_barrier_semaphore()
    each(
        lambda g, i: pl.semaphore_signal(barrier, inc=1, device_id=to(g, i), device_id_type=MESH)
    )
    return barrier


def wait_for(src, dst, n, at, send_sem, recv_sem, peer):
    return pltpu.make_async_remote_copy(
        src_ref=src.at[pl.ds(at, n)], dst_ref=dst.at[pl.ds(at, n)],
        send_sem=send_sem, recv_sem=recv_sem, device_id=peer, device_id_type=MESH,
    )


def forward_kernel(
    table_ref, src_ref, spread_ref,
    seed_ref, idx_ref, meta_ref, slot_ref, kb_ref,
    srcf, rows_f, send, mine, block_v, block_s, recv, mid, mid2, last, kcol,
    ssem, rsem, xs, xr, ys, yr, lsem,
):
    tx, ty, to, from_y = partners()
    me_t, me_q = tx * NY_DEV + ty, ty * NX_DEV + tx
    barrier = greet_all(to)
    meta, block = route(table_ref, slot_ref, kb_ref)
    block_v[...] = block
    fetch = pltpu.make_async_copy(block_v, block_s, lsem.at[3])
    fetch.start()
    for i in range(NX_DEV):
        mine[i] = meta[i * NY_DEV : (i + 1) * NY_DEV, :]
    own_mid = pltpu.make_async_copy(mine.at[tx], mid.at[tx], lsem.at[1])
    own_mid.start()

    @pl.loop(0, OWNED // 128)
    def _(i):
        at = pl.ds(pl.multiple_of(i * 128, 128), 128)
        srcf[at, :] = src_ref[at, :].astype(F32)

    fetch.wait()
    pl.semaphore_wait(barrier, DEV - 1)

    def pack(t):
        for u in range(CAP):
            rows_f[u : u + 1, :] = srcf[pl.ds(block_s[u, t], 1), :]
        send[t] = rows_f[...].astype(BF16)

    def x_copy(i, peer, there):
        return pltpu.make_async_remote_copy(
            src_ref=mine.at[peer], dst_ref=mid.at[there], send_sem=xs.at[i],
            recv_sem=xr.at[i], device_id=(peer, ty), device_id_type=MESH,
        )

    def y_copy(i, peer, there):
        return pltpu.make_async_remote_copy(
            src_ref=mid2.at[peer], dst_ref=last.at[there], send_sem=ys.at[i],
            recv_sem=yr.at[i], device_id=(tx, peer), device_id_type=MESH,
        )


    @pl.loop(1, NX_DEV)
    def _(i):
        x_copy(i, (tx + i) % NX_DEV, tx).start()

    def post(g, i):
        a, b = to(g, i)
        t = a * NY_DEV + b
        pack(t)
        pltpu.make_async_remote_copy(
            src_ref=send.at[t], dst_ref=recv.at[me_q], send_sem=ssem,
            recv_sem=rsem.at[g], device_id=(a, b), device_id_type=MESH,
        ).start()

    each(post, 0, 2)
    own_mid.wait()

    @pl.loop(1, NX_DEV)
    def _(i):
        x_copy(i, (tx + NX_DEV - i) % NX_DEV, (tx + NX_DEV - i) % NX_DEV).wait()

    for j in range(NY_DEV):
        mid2[j] = mid[:, j, :]
    own_meta = pltpu.make_async_copy(mid2.at[ty], last.at[ty], lsem.at[2])
    own_meta.start()

    @pl.loop(1, NY_DEV)
    def _(i):
        y_copy(i, (ty + i) % NY_DEV, ty).start()

    each(post, 2, AHEAD)
    pack(me_t)
    own = pltpu.make_async_copy(send.at[me_t], recv.at[me_q], lsem.at[0])
    own.start()
    own_meta.wait()
    own.wait()

    @pl.loop(1, NY_DEV)
    def _(i):
        y_copy(i, (ty + NY_DEV - i) % NY_DEV, (ty + NY_DEV - i) % NY_DEV).wait()

    meta = last[...].reshape(DEV, 128)
    meta_ref[...] = meta
    idx_ref[...] = meta & 16383
    kind1 = jnp.transpose(((meta >> 14) & 31).astype(F32))[:CAP, :]
    kcol[...] = kind1

    @pl.loop(0, NY_DEV)
    def _(g):
        @pl.when(g < NY_DEV - AHEAD)
        def _():
            for i in range(NX_DEV):
                post(g + AHEAD, i)

        q = from_y(g)

        @pl.when(g == 0)
        def _():
            wait_for(send, recv, NX_DEV - 1, 0, ssem, rsem.at[0], to(0, 1)).wait_recv()

        @pl.when(g > 0)
        def _():
            wait_for(send, recv, NX_DEV, q * NX_DEV, ssem, rsem.at[g], to(0, 1)).wait_recv()

        kinds = pltpu.roll(kcol[...], (DEV - q * NX_DEV) % DEV, 1)
        kb = jnp.concatenate(
            [jnp.broadcast_to(kinds[:, i : i + 1], (CAP, 128)) for i in range(NX_DEV)], axis=0
        ).astype(BF16)
        x = recv[pl.ds(q * NX_DEV, NX_DEV)].reshape(NX_DEV * CAP, 128)
        zero = jnp.zeros_like(x)
        masked = jnp.concatenate(
            [jnp.where(kb == jnp.asarray(k + 1, BF16), x, zero) for k in range(KINDS)], axis=1
        )
        rows = pl.ds(pl.multiple_of(q * (NX_DEV * CAP), NX_DEV * CAP), NX_DEV * CAP)
        seed_ref[rows, :] = dot(masked, spread_ref[...])

    wait_for(send, recv, DEV - 1, 0, ssem, rsem.at[0], to(0, 1)).wait_send()


def scatter_kernel(idx_s, meta_s, seed_ref, *refs):
    fields, acc, held, sem = refs[:3], refs[3], refs[4:7], refs[7]
    loads = [pltpu.make_async_copy(f, h, sem.at[n]) for n, (f, h) in enumerate(zip(fields, held))]
    for load in loads:
        load.start()

    @pl.loop(0, ROWS // 32)
    def _(i):
        acc[pl.ds(pl.multiple_of(i * 32, 32), 32), :] = jnp.zeros((32, 128), F32)

    @pl.loop(0, DEV)
    def _(q):
        count = meta_s[q, CAP]
        for g in range(CAP // GROUP):

            @pl.when(count > g * GROUP)
            def _():
                base = pl.multiple_of(q * CAP + g * GROUP, GROUP)
                at = [pl.ds(idx_s[q, g * GROUP + u], 1) for u in range(GROUP)]
                clash = meta_s[q, g * GROUP + GROUP - 1]

                @pl.when(clash < (1 << 20))
                def _():
                    new = [acc[at[u], :] + seed_ref[pl.ds(base + u, 1), :] for u in range(GROUP)]
                    for u in range(GROUP):
                        acc[at[u], :] = new[u]

                @pl.when(clash >= (1 << 20))
                def _():
                    for u in range(GROUP):
                        acc[at[u], :] = acc[at[u], :] + seed_ref[pl.ds(base + u, 1), :]

    for load in loads:
        load.wait()


def backward_kernel(
    idx_s, cot_ref, cond_ref, diag_ref, add_ref,
    out_ref, recvf,
    rhs, inv, g0, g1, adj, heat, hsend, recv,
    xe, ye, xh, yh,
    ssem, rsem, hs, hr, lsem,
):
    tx, ty, to, from_y = partners()
    me_t, me_q = tx * NY_DEV + ty, ty * NX_DEV + tx
    lane = iota((8, 128), 1)
    barrier = greet_all(to)
    adj[pl.ds(PATCHES, CAP), :] = jnp.zeros((CAP, 128), F32)
    for g in (g0, g1):
        for c in range(CH):
            for l in (0, NZ + 1):

                @pl.loop(0, CX // 64)
                def _(i):
                    g[pl.ds((c * (NZ + 2) + l) * SEG + 8 + i * 64, 64), :] = jnp.zeros((64, 128), F32)

    def cell(c, l, r):
        return l, pl.ds(r, 8), pl.ds(c * 128, 128)

    def row_of(c, l, r):
        return pl.ds(pl.multiple_of(c * (NZ * CX) + l * CX + r, 8), 8)

    def grow_of(c, l, r):
        return pl.multiple_of((c * (NZ + 2) + l + 1) * SEG + 8 + r, 8)

    def edges(acc, lo, hi, j):
        left, right = acc
        left = jnp.where(lane == j, pltpu.roll(lo, j, 1), left)
        right = jnp.where(lane == j, pltpu.roll(hi, (j + 1) % 128, 1), right)
        return left, right

    def visit(body, after=None):
        for h in range(2):

            def step(i, acc):
                for v in range(0, UNROLL, BATCH):
                    stores = []
                    for u in range(v, v + BATCH):
                        j = i * UNROLL + u
                        r = pl.multiple_of((i % (32 // UNROLL)) * (UNROLL * 8), 8) + u * 8
                        writes, lo, hi = body(h * 4 + i // (32 // UNROLL), r, j, h)
                        stores += writes
                        if after is not None:
                            acc = edges(acc, lo, hi, j)
                    for ref, at, value in stores:
                        ref[at] = value
                return acc

            acc = lax.fori_loop(0, 128 // UNROLL, step, (jnp.zeros((8, 128), F32),) * 2)
            if after is not None:
                after(h, acc)

    def keep_edges(s):
        def after(h, acc):
            ye[s, 0, pl.ds(h * 8, 8), :] = acc[0]
            ye[s, 1, pl.ds(h * 8, 8), :] = acc[1]

        return after

    def start(l, r, j, h):
        writes, ends = [], []
        for c in range(CH):
            at = row_of(c, l, r), slice(None)
            q = 1.0 / diag_ref[cell(c, l, r)]
            value = cot_ref[cell(c, l, r)] + add_ref[at]
            g = cond_ref[cell(c, l, r)] * (value * q)
            writes.append((rhs, at, value))
            writes.append((inv, at, q))
            writes.append((g0, (pl.ds(grow_of(c, l, r), 8), slice(None)), g))
            ends.append(g)
        return writes, ends[0], ends[-1]

    def sums(g, s, l, r, j, h):
        own = [g[pl.ds(grow_of(c, l, r), 8), :] for c in range(CH)]
        before = pltpu.roll(yh[s, 0, pl.ds(h * 8, 8), :], 127 - j, 1)
        behind = pltpu.roll(yh[s, 1, pl.ds(h * 8, 8), :], (128 - j) % 128, 1)
        wide = [before, *own, behind]
        out = []
        for c in range(CH):
            b = grow_of(c, l, r)
            west = pltpu.roll(jnp.where(lane == 127, wide[c], own[c]), 1, 1)
            east = pltpu.roll(jnp.where(lane == 0, wide[c + 2], own[c]), 127, 1)
            total = g[pl.ds(b - 1, 8), :] + g[pl.ds(b + 1, 8), :]
            total = total + west + east
            out.append(total + g[pl.ds(b - SEG, 8), :] + g[pl.ds(b + SEG, 8), :])
        return out

    def first(l, r, j, h):
        writes, ends = [], []
        for c, total in enumerate(sums(g0, 0, l, r, j, h)):
            at = row_of(c, l, r), slice(None)
            g = cond_ref[cell(c, l, r)] * ((rhs[at] + total) * inv[at])
            writes.append((g1, (pl.ds(grow_of(c, l, r), 8), slice(None)), g))
            ends.append(g)
        return writes, ends[0], ends[-1]

    def second(l, r, j, h):
        writes = []
        for c, total in enumerate(sums(g1, 1, l, r, j, h)):
            at = row_of(c, l, r), slice(None)
            value = (rhs[at] + total) * inv[at]
            writes.append((adj, at, value))
            writes.append((out_ref, cell(c, l, r), value))
        return writes, None, None

    up, down = (tx + NX_DEV - 1) % NX_DEV, (tx + 1) % NX_DEV
    west, east = (ty + NY_DEV - 1) % NY_DEV, (ty + 1) % NY_DEV

    def halo(s, g):
        for c in range(CH):
            for l in range(NZ):
                n = c * NZ + l
                b = (c * (NZ + 2) + l + 1) * SEG + 8
                xe[s, 0, n : n + 1, :] = g[b : b + 1, :]
                xe[s, 1, n : n + 1, :] = g[b + CX - 1 : b + CX, :]
        if s == 0:
            pl.semaphore_wait(barrier, DEV - 1)
        copies = []
        for i, (src, dst, dev) in enumerate(
            (
                (ye.at[s, 0], yh.at[s, 1], (tx, west)),
                (ye.at[s, 1], yh.at[s, 0], (tx, east)),
                (xe.at[s, 0], xh.at[s, 1], (up, ty)),
                (xe.at[s, 1], xh.at[s, 0], (down, ty)),
            )
        ):
            copies.append(
                pltpu.make_async_remote_copy(
                    src_ref=src, dst_ref=dst, send_sem=hs.at[s, i], recv_sem=hr.at[s, i],
                    device_id=dev, device_id_type=MESH,
                )
            )
            copies[-1].start()
        for copy in copies:
            copy.wait()
        outer = jnp.where(tx == 0, 0.0, xh[s, 0])
        outer2 = jnp.where(tx == NX_DEV - 1, 0.0, xh[s, 1])
        for c in range(CH):
            for l in range(NZ):
                n = c * NZ + l
                b = (c * (NZ + 2) + l + 1) * SEG + 8
                g[b - 1 : b, :] = outer[n : n + 1, :]
                g[b + CX : b + CX + 1, :] = outer2[n : n + 1, :]
        yh[s, 0] = jnp.where(ty == 0, 0.0, yh[s, 0])
        yh[s, 1] = jnp.where(ty == NY_DEV - 1, 0.0, yh[s, 1])

    visit(start, keep_edges(0))
    halo(0, g0)
    visit(first, keep_edges(1))
    halo(1, g1)
    visit(second)

    def take(q):
        for u in range(CAP):
            heat[pl.ds(u, 1), :] = adj[pl.ds(idx_s[q, u], 1), :]
        hsend[q] = heat[...].astype(BF16)

    def post(g, i):
        a, b = to(g, i)
        q = b * NX_DEV + a
        take(q)
        pltpu.make_async_remote_copy(
            src_ref=hsend.at[q], dst_ref=recv.at[me_t], send_sem=ssem,
            recv_sem=rsem, device_id=(a, b), device_id_type=MESH,
        ).start()

    each(post)
    take(me_q)
    own = pltpu.make_async_copy(hsend.at[me_q], recv.at[me_t], lsem)
    own.start()

    own.wait()

    wait_for(hsend, recv, DEV - 1, 0, ssem, rsem, to(0, 1)).wait()

    @pl.loop(0, DEV // 4)
    def _(i):
        recvf[pl.ds(pl.multiple_of(i * 128, 128), 128), :] = (
            recv[pl.ds(i * 4, 4)].reshape(128, 128).astype(F32)
        )


def pull_kernel(slot_s, recvf, kb_ref, spread_ref, deriv_ref, temp_ref, out_ref, grad_ref, even, odd, sem):
    save = pltpu.make_async_copy(temp_ref, out_ref, sem)
    save.start()

    def gather(i, rows):
        for n in range(256):
            rows[n : n + 1, :] = recvf[pl.ds(slot_s[i * 2 + n // 128, n % 128], 1), :]

    def pull(i, rows):
        at = pl.ds(pl.multiple_of(i * 256, 256), 256)
        x = rows[...].astype(BF16)
        kb = kb_ref[at, :]
        zero = jnp.zeros_like(x)
        masked = jnp.concatenate(
            [jnp.where(kb == jnp.asarray(k, BF16), x, zero) for k in range(KINDS)], axis=1
        )
        wide = jnp.concatenate([spread_ref[k] for k in range(KINDS)], axis=1)
        total = lax.dot_general(masked, wide, NT, preferred_element_type=F32)
        grad_ref[at, :] = deriv_ref[at, :] * total

    gather(0, even)

    @pl.loop(0, 4)
    def _(i):
        gather(2 * i + 1, odd)
        pull(2 * i, even)
        gather(jnp.minimum(2 * i + 2, 7), even)
        pull(2 * i + 1, odd)

    save.wait()


def local(cot_field, conductance, diagonal, source_adjoint, spreading, heat_deriv, block_tile, block_patch, block_kind):
    grid16 = (OWNED // 128, 128)
    shape = jax.ShapeDtypeStruct
    dma = pltpu.SemaphoreType.DMA
    seeds, idx, got, slots, kinds = pl.pallas_call(
        forward_kernel,
        out_shape=(
            shape((SLOTS, 128), F32),
            shape((DEV, 128), I32),
            shape((DEV, 128), I32),
            shape(grid16, I32),
            shape((OWNED, 128), BF16),
        ),
        in_specs=[VMEM] * 3,
        out_specs=(VMEM,) * 5,
        scratch_shapes=[
            pltpu.VMEM((OWNED, 128), F32),
            pltpu.VMEM((CAP, 128), F32),
            pltpu.VMEM((DEV, CAP, 128), BF16),
            pltpu.VMEM((NX_DEV, NY_DEV, 128), I32),
            pltpu.VMEM((CAP, DEV), I32),
            pltpu.SMEM((CAP, DEV), I32),
            pltpu.VMEM((DEV, CAP, 128), BF16),
            pltpu.VMEM((NX_DEV, NY_DEV, 128), I32),
            pltpu.VMEM((NY_DEV, NX_DEV, 128), I32),
            pltpu.VMEM((NY_DEV, NX_DEV, 128), I32),
            pltpu.VMEM((CAP, DEV), F32),
            dma,
            dma((NY_DEV,)),
            dma((NX_DEV,)),
            dma((NX_DEV,)),
            dma((NY_DEV,)),
            dma((NY_DEV,)),
            dma((4,)),
        ],
        compiler_params=pltpu.CompilerParams(
            collective_id=0, has_side_effects=True, vmem_limit_bytes=12 << 20
        ),
        name="forward",
    )(
        jnp.concatenate([x.reshape(grid16) for x in (block_tile, block_patch, block_kind)]),
        source_adjoint,
        spreading.reshape(KINDS * 128, 128),
    )

    hbm = pl.BlockSpec(memory_space=pltpu.MemorySpace.HBM)
    added, *fields = pl.pallas_call(
        scatter_kernel,
        out_shape=(shape((ROWS, 128), F32),) + (shape(cot_field.shape, F32),) * 3,
        in_specs=[SMEM, SMEM, VMEM] + [hbm] * 3,
        out_specs=(VMEM,) * 4,
        scratch_shapes=[dma((3,))],
        compiler_params=pltpu.CompilerParams(vmem_limit_bytes=36 << 20),
        name="scatter",
    )(idx, got, seeds, cot_field, conductance, diagonal)

    flat = pltpu.VMEM((PATCHES, 128), F32)
    padded = pltpu.VMEM((GROWS, 128), F32)
    temp, heat = pl.pallas_call(
        backward_kernel,
        out_shape=(shape(cot_field.shape, F32), shape((SLOTS, 128), F32)),
        in_specs=[SMEM] + [VMEM] * 4,
        out_specs=(VMEM, VMEM),
        scratch_shapes=[
            flat,
            flat,
            padded,
            padded,
            pltpu.VMEM((ROWS, 128), F32),
            pltpu.VMEM((CAP, 128), F32),
            pltpu.VMEM((DEV, CAP, 128), BF16),
            pltpu.VMEM((DEV, CAP, 128), BF16),
            pltpu.VMEM((2, 2, CH * NZ, 128), F32),
            pltpu.VMEM((2, 2, 16, 128), F32),
            pltpu.VMEM((2, 2, CH * NZ, 128), F32),
            pltpu.VMEM((2, 2, 16, 128), F32),
            dma,
            dma,
            dma((2, 4)),
            dma((2, 4)),
            dma,
        ],
        compiler_params=pltpu.CompilerParams(
            collective_id=1, has_side_effects=True, vmem_limit_bytes=30 << 20
        ),
        name="backward",
    )(idx, *fields, added)

    return pl.pallas_call(
        pull_kernel,
        out_shape=(shape(cot_field.shape, F32), shape((OWNED, 128), F32)),
        in_specs=[SMEM, VMEM, VMEM, VMEM, VMEM, VMEM],
        out_specs=(ANY, VMEM),
        scratch_shapes=[pltpu.VMEM((256, 128), F32), pltpu.VMEM((256, 128), F32), dma],
        compiler_params=pltpu.CompilerParams(vmem_limit_bytes=16 << 20),
        name="pull",
    )(slots, heat, kinds, spreading, heat_deriv, temp)


def solution(mesh):
    blocks = P(("tx", "ty"))
    field = P(None, "tx", "ty")
    in_specs = (
        field, field, field, P(("tx", "ty"), None), P(), P(("tx", "ty"), None),
        P(("tx", "ty"), None), blocks, blocks,
    )
    out_specs = (field, P(("tx", "ty"), None))
    return jax.shard_map(local, mesh=mesh, in_specs=in_specs, out_specs=out_specs, check_vma=False)
```

time: 133 us -> 114 us (0.86)
  Pallas kernels: 124 us -> 108 us
  local copies, waits for them, and re-layouts: 7.26 us -> 4.28 us
    pallas_call x1, Pallas kernels: 59.6 us -> 50.7 us  [local(): pl.pallas_call(backward_kernel, out_shape=(shape(cot_field.shape, F32), s...]
    pallas_call x2, Pallas kernels: 25.1 us -> 19.8 us  [the longest x1 13.7 us: local(): pl.pallas_call(scatter_kernel, out_shape=(shape((ROWS, 128), F32),) + (sh...]
    unnamed x16 -> x10, local copies, waits for them, and re-layouts: 7.26 us -> 4.28 us
    pallas_call x1, Pallas kernels: 39.5 us -> 37.2 us  [local(): pl.pallas_call(forward_kernel, out_shape=(shape((SLOTS, 128), F32), shape...]
where the time goes in v3:
time: 114 us; the launch traced here: 113 us
  Pallas kernels  108 us (95%)
  local copies, waits for them, and re-layouts  4.28 us (4%)
    pallas_call x1, Pallas kernels, local(): pl.pallas_call(backward_kernel, out_shape=(shape(cot_field.shape, F32), s...  50.7 us
    pallas_call x1, Pallas kernels, local(): pl.pallas_call(forward_kernel, out_shape=(shape((SLOTS, 128), F32), shape...  37.2 us
    pallas_call x1, Pallas kernels, local(): pl.pallas_call(scatter_kernel, out_shape=(shape((ROWS, 128), F32),) + (sh...  13.7 us
    pallas_call x1, Pallas kernels, local(): pl.pallas_call(pull_kernel, out_shape=(shape(cot_field.shape, F32), shape...  6.09 us
    unnamed x10, local copies, waits for them, and re-layouts  4.28 us

profile of v3, /device:TPU:1, one launch (start us, length us, event | category | flops | bytes accessed | tf_op | source)
XLA Modules:
  0.0 113.4 jit_solution(4962137408801390693)
XLA Ops:
  0.6 0.7 pad_add_fusion.table_ref
  1.4 0.0 copy-start.1
  1.4 1.0 copy-done.1
  2.4 0.0 copy-start.4
  2.4 1.0 copy-done.4
  3.4 37.2 %forward.1 = (f32[4096,128]{1,0:T(8,128)S(1)}, s32[128,128]{1,0:T(8,128)S(1)}, s32[128,128]{1,0:T(8,128)S(1)}, s32[16,128]{1,0:T(8,128)S(1)}, bf16[2048,128]{1,0:T(8,128)(2,1)S(1)}) custom-call(s32[48,128]{1,0:T(8,128)S(1)} %pad_add_fusion.table_ref, bf16[2048,128]{1,0:T(8,128)(2,1)S(1)} %copy-done.4, bf16[2048,128]{1,0:T(8,128)(2,1)S(1)} %bitcast.4), custom_call_target="tpu_custom_call" | custom-call | tf_op jit(solution)/shard_map/forward/pallas_call | solution.py:508
  40.7 13.7 %scatter.1 = (f32[8224,128]{1,0:T(8,128)}, f32[8,256,512]{2,1,0:T(8,128)S(1)}, f32[8,256,512]{2,1,0:T(8,128)S(1)}, f32[8,256,512]{2,1,0:T(8,128)S(1)}) custom-call(s32[128,128]{1,0:T(8,128)S(1)} %get-tuple-element.14.idx_s, s32[128,128]{1,0:T(8,128)S(1)} %get-tuple-element.15.meta_s, f32[4096,128]{1,0:T(8,128)S(1)} %get-tuple-element.16.seed_ref, ...), custom_call_target="tpu_custom_call" | custom-call | tf_op jit(solution)/shard_map/scatter/pallas_call | solution.py:550
  54.4 0.0 copy-start
  54.4 2.2 %copy-done = f32[8224,128]{1,0:T(8,128)S(1)} copy-done((f32[8224,128]{1,0:T(8,128)S(1)}, f32[8224,128]{1,0:T(8,128)}, u32[]{:S(2)}) %copy-start) | copy-done | bytes 4210712
  56.6 0.0 copy-start.2
  56.6 0.0 copy-start.3
  56.6 50.7 %backward.1 = (f32[8,256,512]{2,1,0:T(8,128)S(1)}, f32[4096,128]{1,0:T(8,128)S(1)}) custom-call(s32[128,128]{1,0:T(8,128)S(1)} %get-tuple-element.14.idx_s, f32[8,256,512]{2,1,0:T(8,128)S(1)} %get-tuple-element.17.cot_ref, f32[8,256,512]{2,1,0:T(8,128)S(1)} %get-tuple-element.18.cond_ref, f32[8,256,512]{2,1,0:T(8,128)S(1)} %get-tuple-element.19.diag_ref, ...), custom_call_target="tpu_custom_call" | custom-call | tf_op jit(solution)/shard_map/backward/pallas_call | solution.py:562
  107.3 0.0 copy-done.2
  107.3 0.0 copy-done.3
  107.3 6.1 %pull.1 = (f32[8,256,512]{2,1,0:T(8,128)}, f32[2048,128]{1,0:T(8,128)}) custom-call(s32[16,128]{1,0:T(8,128)S(1)} %get-tuple-element.13.slot_s, f32[4096,128]{1,0:T(8,128)S(1)} %get-tuple-element.21.recvf, bf16[2048,128]{1,0:T(8,128)(2,1)S(1)} %get-tuple-element.22.kb_ref, bf16[16,128,128]{2,1,0:T(8,128)(2,1)S(1)} %copy-done.2, f32[2048,128]{1,0:T(8,128)S(1)} %copy-done.3, ...), custom_call_target="tpu_custom_call" | custom-call | tf_op jit(solution)/shard_map/pull/pallas_call | solution.py:592
Async XLA Ops:
  1.4 1.0 copy-start.1
  2.4 1.0 copy-start.4
  54.4 2.2 %copy-start = (f32[8224,128]{1,0:T(8,128)S(1)}, f32[8224,128]{1,0:T(8,128)}, u32[]{:S(2)}) copy-start(f32[8224,128]{1,0:T(8,128)} %get-tuple-element.20.add_ref) | copy-start | bytes 12632068
  56.6 50.7 %copy-start.2 = (bf16[16,128,128]{2,1,0:T(8,128)(2,1)S(1)}, bf16[16,128,128]{2,1,0:T(8,128)(2,1)}, u32[]{:S(2)}) copy-start(bf16[16,128,128]{2,1,0:T(8,128)(2,1)} %spread_ref.1) | copy-start | bytes 1572868
  56.6 50.7 %copy-start.3 = (f32[2048,128]{1,0:T(8,128)S(1)}, f32[2048,128]{1,0:T(8,128)}, u32[]{:S(2)}) copy-start(f32[2048,128]{1,0:T(8,128)} %deriv_ref.1) | copy-start | bytes 3145732

commit v4 on v3

--- a/solution.py
+++ b/solution.py
@@ -20,6 +20,7 @@
 GROWS = CH * (NZ + 2) * SEG
 OWNED = 2048
 GROUP = 8
+CLASH = 8
 AHEAD = 6
 UNROLL, BATCH = 16, 1
 F32, BF16, I32 = jnp.float32, jnp.bfloat16, jnp.int32
@@ -75,16 +76,13 @@
     place = (held * 128.0 + pltpu.roll(held, 128 - CAP, 1)).astype(I32)
     kind1 = pltpu.roll(held, 128 - 2 * CAP, 1).astype(I32)
     place = jnp.where(lane < counts, place, PATCHES + lane)
-    within = lane & (GROUP - 1)
     clash = jnp.zeros((128, 128), I32)
-    for k in range(1, GROUP):
-        same = (pltpu.roll(place, k, 1) == place) & (within >= k)
+    for k in range(1, CAP):
+        same = (pltpu.roll(place, k, 1) == place) & (lane >= k) & (lane < counts)
         clash = jnp.maximum(clash, same.astype(I32))
-    for k in (1, 2, 4, 8):
-        if k < GROUP:
-            clash = jnp.maximum(clash, jnp.where(within >= k, pltpu.roll(clash, k, 1), 0))
-    meta = place + kind1 * 16384 + clash * (1 << 20)
-    return jnp.where(lane < CAP, meta, counts), block.astype(I32) & (OWNED - 1)
+    clash = jnp.max(clash, axis=1, keepdims=True)
+    groups = (counts + (GROUP - 1)) // GROUP + clash * CLASH
+    return jnp.where(lane < CAP, place + kind1 * 16384, groups), block.astype(I32) & (OWNED - 1)
 
 
 def partners():
@@ -259,25 +257,22 @@
 
     @pl.loop(0, DEV)
     def _(q):
-        count = meta_s[q, CAP]
-        for g in range(CAP // GROUP):
-
-            @pl.when(count > g * GROUP)
+        groups = meta_s[q, CAP]
+        base = pl.multiple_of(q * CAP, CAP)
+        for n in range(1, CAP // GROUP + 1):
+
+            @pl.when(groups == n)
             def _():
-                base = pl.multiple_of(q * CAP + g * GROUP, GROUP)
-                at = [pl.ds(idx_s[q, g * GROUP + u], 1) for u in range(GROUP)]
-                clash = meta_s[q, g * GROUP + GROUP - 1]
-
-                @pl.when(clash < (1 << 20))
-                def _():
-                    new = [acc[at[u], :] + seed_ref[pl.ds(base + u, 1), :] for u in range(GROUP)]
-                    for u in range(GROUP):
-                        acc[at[u], :] = new[u]
-
-                @pl.when(clash >= (1 << 20))
-                def _():
-                    for u in range(GROUP):
-                        acc[at[u], :] = acc[at[u], :] + seed_ref[pl.ds(base + u, 1), :]
+                at = [pl.ds(idx_s[q, u], 1) for u in range(n * GROUP)]
+                new = [acc[at[u], :] + seed_ref[pl.ds(base + u, 1), :] for u in range(n * GROUP)]
+                for u in range(n * GROUP):
+                    acc[at[u], :] = new[u]
+
+        @pl.when(groups > CLASH)
+        def _():
+            for u in range(CAP):
+                at = pl.ds(idx_s[q, u], 1)
+                acc[at, :] = acc[at, :] + seed_ref[pl.ds(base + u, 1), :]
 
     for load in loads:
         load.wait()

time: 114 us -> 113 us (level)
    pallas_call x1, Pallas kernels: 50.7 us -> 49.3 us  [local(): pl.pallas_call(backward_kernel, out_shape=(shape(cot_field.shape, F32), s...]
where the time goes in v4:
time: 113 us
  Pallas kernels  107 us (95%)
  local copies, waits for them, and re-layouts  4.28 us (4%)
    pallas_call x1, Pallas kernels, local(): pl.pallas_call(backward_kernel, out_shape=(shape(cot_field.shape, F32), s...  49.3 us
    pallas_call x1, Pallas kernels, local(): pl.pallas_call(forward_kernel, out_shape=(shape((SLOTS, 128), F32), shape...  37.2 us
    pallas_call x1, Pallas kernels, local(): pl.pallas_call(scatter_kernel, out_shape=(shape((ROWS, 128), F32),) + (sh...  14.3 us
    pallas_call x1, Pallas kernels, local(): pl.pallas_call(pull_kernel, out_shape=(shape(cot_field.shape, F32), shape...  6.1 us
    unnamed x10, local copies, waits for them, and re-layouts  4.28 us

profile of v4, /device:TPU:1, one launch (start us, length us, event | category | flops | bytes accessed | tf_op | source)
XLA Modules:
  0.0 112.6 jit_solution(9553463065830243417)
XLA Ops:
  0.6 0.7 pad_add_fusion.table_ref
  1.4 0.0 copy-start.1
  1.4 1.0 copy-done.1
  2.4 0.0 copy-start.4
  2.4 1.0 copy-done.4
  3.4 37.2 %forward.1 = (f32[4096,128]{1,0:T(8,128)S(1)}, s32[128,128]{1,0:T(8,128)S(1)}, s32[128,128]{1,0:T(8,128)S(1)}, s32[16,128]{1,0:T(8,128)S(1)}, bf16[2048,128]{1,0:T(8,128)(2,1)S(1)}) custom-call(s32[48,128]{1,0:T(8,128)S(1)} %pad_add_fusion.table_ref, bf16[2048,128]{1,0:T(8,128)(2,1)S(1)} %copy-done.4, bf16[2048,128]{1,0:T(8,128)(2,1)S(1)} %bitcast.4), custom_call_target="tpu_custom_call" | custom-call | tf_op jit(solution)/shard_map/forward/pallas_call | solution.py:503
  40.7 14.3 %scatter.1 = (f32[8224,128]{1,0:T(8,128)}, f32[8,256,512]{2,1,0:T(8,128)S(1)}, f32[8,256,512]{2,1,0:T(8,128)S(1)}, f32[8,256,512]{2,1,0:T(8,128)S(1)}) custom-call(s32[128,128]{1,0:T(8,128)S(1)} %get-tuple-element.14.idx_s, s32[128,128]{1,0:T(8,128)S(1)} %get-tuple-element.15.meta_s, f32[4096,128]{1,0:T(8,128)S(1)} %get-tuple-element.16.seed_ref, ...), custom_call_target="tpu_custom_call" | custom-call | tf_op jit(solution)/shard_map/scatter/pallas_call | solution.py:545
  55.0 0.0 copy-start
  55.0 2.2 %copy-done = f32[8224,128]{1,0:T(8,128)S(1)} copy-done((f32[8224,128]{1,0:T(8,128)S(1)}, f32[8224,128]{1,0:T(8,128)}, u32[]{:S(2)}) %copy-start) | copy-done | bytes 4210712
  57.2 0.0 copy-start.2
  57.2 0.0 copy-start.3
  57.2 49.3 %backward.1 = (f32[8,256,512]{2,1,0:T(8,128)S(1)}, f32[4096,128]{1,0:T(8,128)S(1)}) custom-call(s32[128,128]{1,0:T(8,128)S(1)} %get-tuple-element.14.idx_s, f32[8,256,512]{2,1,0:T(8,128)S(1)} %get-tuple-element.17.cot_ref, f32[8,256,512]{2,1,0:T(8,128)S(1)} %get-tuple-element.18.cond_ref, f32[8,256,512]{2,1,0:T(8,128)S(1)} %get-tuple-element.19.diag_ref, ...), custom_call_target="tpu_custom_call" | custom-call | tf_op jit(solution)/shard_map/backward/pallas_call | solution.py:557
  106.4 0.0 copy-done.2
  106.5 0.0 copy-done.3
  106.5 6.1 %pull.1 = (f32[8,256,512]{2,1,0:T(8,128)}, f32[2048,128]{1,0:T(8,128)}) custom-call(s32[16,128]{1,0:T(8,128)S(1)} %get-tuple-element.13.slot_s, f32[4096,128]{1,0:T(8,128)S(1)} %get-tuple-element.21.recvf, bf16[2048,128]{1,0:T(8,128)(2,1)S(1)} %get-tuple-element.22.kb_ref, bf16[16,128,128]{2,1,0:T(8,128)(2,1)S(1)} %copy-done.2, f32[2048,128]{1,0:T(8,128)S(1)} %copy-done.3, ...), custom_call_target="tpu_custom_call" | custom-call | tf_op jit(solution)/shard_map/pull/pallas_call | solution.py:587
Async XLA Ops:
  1.4 1.0 copy-start.1
  2.4 1.0 copy-start.4
  55.0 2.2 %copy-start = (f32[8224,128]{1,0:T(8,128)S(1)}, f32[8224,128]{1,0:T(8,128)}, u32[]{:S(2)}) copy-start(f32[8224,128]{1,0:T(8,128)} %get-tuple-element.20.add_ref) | copy-start | bytes 12632068
  57.2 49.3 %copy-start.2 = (bf16[16,128,128]{2,1,0:T(8,128)(2,1)S(1)}, bf16[16,128,128]{2,1,0:T(8,128)(2,1)}, u32[]{:S(2)}) copy-start(bf16[16,128,128]{2,1,0:T(8,128)(2,1)} %spread_ref.1) | copy-start | bytes 1572868
  57.2 49.3 %copy-start.3 = (f32[2048,128]{1,0:T(8,128)S(1)}, f32[2048,128]{1,0:T(8,128)}, u32[]{:S(2)}) copy-start(f32[2048,128]{1,0:T(8,128)} %deriv_ref.1) | copy-start | bytes 3145732

commit v5 on v4

--- a/solution.py
+++ b/solution.py
@@ -97,15 +97,17 @@
     return tx, ty, to, from_y
 
 
-def each(do, lo=0, hi=NY_DEV):
+def each(*steps, lo=0, hi=NY_DEV):
     if lo == 0:
-        for i in range(1, NX_DEV):
-            do(0, i)
+        for step in steps:
+            for i in range(1, NX_DEV):
+                step(0, i)
 
     @pl.loop(max(lo, 1), hi)
     def _(g):
-        for i in range(NX_DEV):
-            do(g, i)
+        for step in steps:
+            for i in range(NX_DEV):
+                step(g, i)
 
 
 def greet_all(to):
@@ -149,10 +151,10 @@
     fetch.wait()
     pl.semaphore_wait(barrier, DEV - 1)
 
-    def pack(t):
+    def pack(t, i):
         for u in range(CAP):
-            rows_f[u : u + 1, :] = srcf[pl.ds(block_s[u, t], 1), :]
-        send[t] = rows_f[...].astype(BF16)
+            rows_f[i, u : u + 1, :] = srcf[pl.ds(block_s[u, t], 1), :]
+        send[t] = rows_f[i].astype(BF16)
 
     def x_copy(i, peer, there):
         return pltpu.make_async_remote_copy(
@@ -171,16 +173,16 @@
     def _(i):
         x_copy(i, (tx + i) % NX_DEV, tx).start()
 
-    def post(g, i):
+    def send_one(g, i):
         a, b = to(g, i)
         t = a * NY_DEV + b
-        pack(t)
+        pack(t, i)
         pltpu.make_async_remote_copy(
             src_ref=send.at[t], dst_ref=recv.at[me_q], send_sem=ssem,
             recv_sem=rsem.at[g], device_id=(a, b), device_id_type=MESH,
         ).start()
 
-    each(post, 0, 2)
+    each(send_one, lo=0, hi=2)
     own_mid.wait()
 
     @pl.loop(1, NX_DEV)
@@ -196,8 +198,8 @@
     def _(i):
         y_copy(i, (ty + i) % NY_DEV, ty).start()
 
-    each(post, 2, AHEAD)
-    pack(me_t)
+    each(send_one, lo=2, hi=AHEAD)
+    pack(me_t, 0)
     own = pltpu.make_async_copy(send.at[me_t], recv.at[me_q], lsem.at[0])
     own.start()
     own_meta.wait()
@@ -218,7 +220,7 @@
         @pl.when(g < NY_DEV - AHEAD)
         def _():
             for i in range(NX_DEV):
-                post(g + AHEAD, i)
+                send_one(g + AHEAD, i)
 
         q = from_y(g)
 
@@ -287,9 +289,10 @@
 ):
     tx, ty, to, from_y = partners()
     me_t, me_q = tx * NY_DEV + ty, ty * NX_DEV + tx
+    fetch = pltpu.make_async_copy(add_ref, adj, lsem)
+    fetch.start()
     lane = iota((8, 128), 1)
     barrier = greet_all(to)
-    adj[pl.ds(PATCHES, CAP), :] = jnp.zeros((CAP, 128), F32)
     for g in (g0, g1):
         for c in range(CH):
             for l in (0, NZ + 1):
@@ -346,7 +349,7 @@
         for c in range(CH):
             at = row_of(c, l, r), slice(None)
             q = 1.0 / diag_ref[cell(c, l, r)]
-            value = cot_ref[cell(c, l, r)] + add_ref[at]
+            value = cot_ref[cell(c, l, r)] + adj[at]
             g = cond_ref[cell(c, l, r)] * (value * q)
             writes.append((rhs, at, value))
             writes.append((inv, at, q))
@@ -428,28 +431,31 @@
         yh[s, 0] = jnp.where(ty == 0, 0.0, yh[s, 0])
         yh[s, 1] = jnp.where(ty == NY_DEV - 1, 0.0, yh[s, 1])
 
+    fetch.wait()
     visit(start, keep_edges(0))
     halo(0, g0)
     visit(first, keep_edges(1))
     halo(1, g1)
     visit(second)
 
-    def take(q):
+    def take(q, i):
         for u in range(CAP):
-            heat[pl.ds(u, 1), :] = adj[pl.ds(idx_s[q, u], 1), :]
-        hsend[q] = heat[...].astype(BF16)
+            heat[i, u : u + 1, :] = adj[pl.ds(idx_s[q, u], 1), :]
+        hsend[q] = heat[i].astype(BF16)
+
+    def ready(g, i):
+        a, b = to(g, i)
+        take(b * NX_DEV + a, i)
 
     def post(g, i):
         a, b = to(g, i)
-        q = b * NX_DEV + a
-        take(q)
         pltpu.make_async_remote_copy(
-            src_ref=hsend.at[q], dst_ref=recv.at[me_t], send_sem=ssem,
+            src_ref=hsend.at[b * NX_DEV + a], dst_ref=recv.at[me_t], send_sem=ssem,
             recv_sem=rsem, device_id=(a, b), device_id_type=MESH,
         ).start()
 
-    each(post)
-    take(me_q)
+    each(ready, post)
+    take(me_q, 0)
     own = pltpu.make_async_copy(hsend.at[me_q], recv.at[me_t], lsem)
     own.start()
 
@@ -513,7 +519,7 @@
         out_specs=(VMEM,) * 5,
         scratch_shapes=[
             pltpu.VMEM((OWNED, 128), F32),
-            pltpu.VMEM((CAP, 128), F32),
+            pltpu.VMEM((NX_DEV, CAP, 128), F32),
             pltpu.VMEM((DEV, CAP, 128), BF16),
             pltpu.VMEM((NX_DEV, NY_DEV, 128), I32),
             pltpu.VMEM((CAP, DEV), I32),
@@ -557,7 +563,7 @@
     temp, heat = pl.pallas_call(
         backward_kernel,
         out_shape=(shape(cot_field.shape, F32), shape((SLOTS, 128), F32)),
-        in_specs=[SMEM] + [VMEM] * 4,
+        in_specs=[SMEM] + [VMEM] * 3 + [ANY],
         out_specs=(VMEM, VMEM),
         scratch_shapes=[
             flat,
@@ -565,7 +571,7 @@
             padded,
             padded,
             pltpu.VMEM((ROWS, 128), F32),
-            pltpu.VMEM((CAP, 128), F32),
+            pltpu.VMEM((NX_DEV, CAP, 128), F32),
             pltpu.VMEM((DEV, CAP, 128), BF16),
             pltpu.VMEM((DEV, CAP, 128), BF16),
             pltpu.VMEM((2, 2, CH * NZ, 128), F32),
@@ -579,7 +585,7 @@
             dma,
         ],
         compiler_params=pltpu.CompilerParams(
-            collective_id=1, has_side_effects=True, vmem_limit_bytes=30 << 20
+            collective_id=1, has_side_effects=True, vmem_limit_bytes=33 << 20
         ),
         name="backward",
     )(idx, *fields, added)

time: 113 us -> 111 us (0.982)
  local copies, waits for them, and re-layouts: 4.28 us -> 2.09 us
    pallas_call x1, Pallas kernels: 49.3 us -> 44.2 us  [local(): pl.pallas_call(backward_kernel, out_shape=(shape(cot_field.shape, F32), s...]
    pallas_call x1, Pallas kernels: 14.3 us -> 19.1 us  [local(): pl.pallas_call(scatter_kernel, out_shape=(shape((ROWS, 128), F32),) + (sh...]
    unnamed x10 -> x8, local copies, waits for them, and re-layouts: 4.28 us -> 2.09 us
where the time goes in v5:
time: 111 us; the launch traced here: 110 us
  Pallas kernels  107 us (96%)
  local copies, waits for them, and re-layouts  2.09 us (2%)
    pallas_call x1, Pallas kernels, local(): pl.pallas_call(backward_kernel, out_shape=(shape(cot_field.shape, F32), s...  44.2 us
    pallas_call x1, Pallas kernels, local(): pl.pallas_call(forward_kernel, out_shape=(shape((SLOTS, 128), F32), shape...  37.2 us
    pallas_call x1, Pallas kernels, local(): pl.pallas_call(scatter_kernel, out_shape=(shape((ROWS, 128), F32),) + (sh...  19.1 us
    pallas_call x1, Pallas kernels, local(): pl.pallas_call(pull_kernel, out_shape=(shape(cot_field.shape, F32), shape...  6.1 us

profile of v5, /device:TPU:1, one launch (start us, length us, event | category | flops | bytes accessed | tf_op | source)
XLA Modules:
  0.0 110.2 jit_solution(6494502867646221276)
XLA Ops:
  0.6 0.7 pad_add_fusion.table_ref
  1.4 0.0 copy-start
  1.4 1.0 copy-done
  2.4 0.0 copy-start.3
  2.4 1.0 copy-done.3
  3.4 37.2 %forward.1 = (f32[4096,128]{1,0:T(8,128)S(1)}, s32[128,128]{1,0:T(8,128)S(1)}, s32[128,128]{1,0:T(8,128)S(1)}, s32[16,128]{1,0:T(8,128)S(1)}, bf16[2048,128]{1,0:T(8,128)(2,1)S(1)}) custom-call(s32[48,128]{1,0:T(8,128)S(1)} %pad_add_fusion.table_ref, bf16[2048,128]{1,0:T(8,128)(2,1)S(1)} %copy-done.3, bf16[2048,128]{1,0:T(8,128)(2,1)S(1)} %bitcast.4), custom_call_target="tpu_custom_call" | custom-call | tf_op jit(solution)/shard_map/forward/pallas_call | solution.py:509
  40.7 19.1 %scatter.1 = (f32[8224,128]{1,0:T(8,128)}, f32[8,256,512]{2,1,0:T(8,128)S(1)}, f32[8,256,512]{2,1,0:T(8,128)S(1)}, f32[8,256,512]{2,1,0:T(8,128)S(1)}) custom-call(s32[128,128]{1,0:T(8,128)S(1)} %get-tuple-element.14.idx_s, s32[128,128]{1,0:T(8,128)S(1)} %get-tuple-element.15.meta_s, f32[4096,128]{1,0:T(8,128)S(1)} %get-tuple-element.16.seed_ref, ...), custom_call_target="tpu_custom_call" | custom-call | tf_op jit(solution)/shard_map/scatter/pallas_call | solution.py:551
  59.8 0.0 copy-start.1
  59.9 0.0 copy-start.2
  59.9 44.2 %backward.1 = (f32[8,256,512]{2,1,0:T(8,128)S(1)}, f32[4096,128]{1,0:T(8,128)S(1)}) custom-call(s32[128,128]{1,0:T(8,128)S(1)} %get-tuple-element.14.idx_s, f32[8,256,512]{2,1,0:T(8,128)S(1)} %get-tuple-element.17.cot_ref, f32[8,256,512]{2,1,0:T(8,128)S(1)} %get-tuple-element.18.cond_ref, f32[8,256,512]{2,1,0:T(8,128)S(1)} %get-tuple-element.19.diag_ref, ...), custom_call_target="tpu_custom_call" | custom-call | tf_op jit(solution)/shard_map/backward/pallas_call | solution.py:563
  104.1 0.0 copy-done.1
  104.1 0.0 copy-done.2
  104.1 6.1 %pull.1 = (f32[8,256,512]{2,1,0:T(8,128)}, f32[2048,128]{1,0:T(8,128)}) custom-call(s32[16,128]{1,0:T(8,128)S(1)} %get-tuple-element.13.slot_s, f32[4096,128]{1,0:T(8,128)S(1)} %get-tuple-element.21.recvf, bf16[2048,128]{1,0:T(8,128)(2,1)S(1)} %get-tuple-element.22.kb_ref, bf16[16,128,128]{2,1,0:T(8,128)(2,1)S(1)} %copy-done.1, f32[2048,128]{1,0:T(8,128)S(1)} %copy-done.2, ...), custom_call_target="tpu_custom_call" | custom-call | tf_op jit(solution)/shard_map/pull/pallas_call | solution.py:593
Async XLA Ops:
  1.4 1.0 copy-start
  2.4 1.0 copy-start.3
  59.8 44.3 %copy-start.1 = (bf16[16,128,128]{2,1,0:T(8,128)(2,1)S(1)}, bf16[16,128,128]{2,1,0:T(8,128)(2,1)}, u32[]{:S(2)}) copy-start(bf16[16,128,128]{2,1,0:T(8,128)(2,1)} %spread_ref.1) | copy-start | bytes 1572868
  59.9 44.3 %copy-start.2 = (f32[2048,128]{1,0:T(8,128)S(1)}, f32[2048,128]{1,0:T(8,128)}, u32[]{:S(2)}) copy-start(f32[2048,128]{1,0:T(8,128)} %deriv_ref.1) | copy-start | bytes 3145732
